TPU v7x, 256 devices: a whole 4x4x8 slice. The times are simulated.
256 devices in a mesh: section: 16 (over z, y_hi), dp: 16 (over y_lo, x, core).
Axes of the slice: x: 4, y: 4 (y_hi: 2, y_lo: 2; y = y_hi * 2 + y_lo), z: 8, core: 2. Of those that a mesh axis runs over, the one named last changes fastest.
Arguments:
- tokens: bfloat16 [8, 256, 8192], P(None, 'dp'), may hold values from -6 to 6
- cotangent: bfloat16 [8, 256, 8192], P(None, 'dp'), may hold values from -0.119628906 to 0.119628906
- sample_ids: int32 [16, 8], P('dp'), may hold values from 0 to 7, each once within a row
- sent_before: bfloat16 [16, 128, 16, 8192], P('section', 'dp'), may hold values from -1.796875 to 1.796875
- received_before: bfloat16 [16, 128, 16, 8192], P('section', 'dp'), may hold values from -1.796875 to 1.796875
- norm_gain: float32 [16, 8192], P('section'), may hold values from 0.5 to 2
- down_proj: bfloat16 [16, 8192, 256], P('section', 'dp'), may hold values from -0.0625 to 0.0625
- up_proj: bfloat16 [16, 256, 8192], P('section', None, 'dp'), may hold values from -0.375 to 0.375
Outputs:
- grad_down: float32 [16, 8192, 256], P('section', 'dp')
- grad_up: float32 [16, 256, 8192], P('section', None, 'dp')
Inputs may be any that keep to these rules, and one draw needn't show every extreme that they name: Each row of sample_ids, one replica's micro-batches, names each of its 8 stored samples once.
All inputs are finite; a program needn't handle non-finite values.
Results may differ from a plain program's by a relative error of at most 0.035.
Values may be sent and summed in bfloat16 or wider, within the bound.
A program may use at most 128 MiB of HBM per device.

v0:
```python
import jax
import jax.numpy as jnp
from jax import lax
from jax.sharding import PartitionSpec as P

epsilon = 1e-05


def shifted(value, axis, steps):
    count = lax.axis_size(axis)
    leading, last = (max(0, -steps), min(count, count - steps))
    return lax.ppermute(value, axis, [(source, source + steps) for source in range(leading, last)])


def normalize(activation, gain_row, down_weight):
    row_scale = lax.rsqrt(jnp.mean(activation * activation, axis=-1, keepdims=True) + epsilon)
    normed = (activation * row_scale * gain_row).astype(jnp.bfloat16)
    pre_act = jnp.dot(normed, down_weight, preferred_element_type=jnp.float32)
    active = jax.nn.silu(pre_act).astype(jnp.bfloat16)
    return (row_scale, normed, pre_act, active)


def transposed(operand_a, operand_b):
    return lax.dot_general(
        operand_a, operand_b, (((1,), (1,)), ((), ())), preferred_element_type=jnp.float32
    )


def over_rows(operand_a, operand_b):
    return lax.dot_general(
        operand_a, operand_b, (((0,), (0,)), ((), ())), preferred_element_type=jnp.float32
    )


def backward_layer(activation, upstream, gain_row, down_weight, up_weight):
    row_scale, normed, pre_act, active = normalize(activation, gain_row, down_weight)
    upstream_b = upstream.astype(jnp.bfloat16)
    d_active = transposed(upstream_b, up_weight)
    gate_sig = jax.nn.sigmoid(pre_act)
    d_pre = (d_active * gate_sig * (1.0 + pre_act * (1.0 - gate_sig))).astype(jnp.bfloat16)
    d_normed = transposed(d_pre, down_weight) * gain_row
    d_state = (
        upstream
        + row_scale * d_normed
        - activation * row_scale**3 * jnp.mean(d_normed * activation, axis=-1, keepdims=True)
    )
    return (d_state, normed, active, upstream_b, d_pre)


def shards(
    tokens, cotangent, sample_ids, sent_before, received_before, norm_gain, down_proj, up_proj
):
    section_count = lax.axis_size("section")
    my_section = lax.axis_index("section")
    micro_count, row_count, feature_count = tokens.shape
    gain_row = norm_gain[0]
    sample_slots = sample_ids[0]
    down_all, up_all = (
        lax.all_gather(down_proj, "dp", axis=1, tiled=True),
        lax.all_gather(up_proj, "dp", axis=2, tiled=True),
    )
    down_weight = down_all[0]
    up_weight = up_all[0]
    rank_count = down_weight.shape[1]
    sent_rows = sent_before[0]
    kept_table = received_before[0]
    turn_count = micro_count + section_count - 1

    def forward_turn(step_now, loop_state):
        incoming, stored_inputs = loop_state
        micro_now = step_now - my_section
        is_live = jnp.logical_and(micro_now >= 0, micro_now < micro_count)
        micro_pick = jnp.clip(micro_now, 0, micro_count - 1)
        slot_pick = sample_slots[micro_pick]

        def advance(unused):
            fresh_rows = lax.dynamic_index_in_dim(tokens, micro_pick, 0, keepdims=False).astype(
                jnp.float32
            )
            stored_rows = lax.dynamic_index_in_dim(kept_table, slot_pick, 0, keepdims=False).astype(
                jnp.float32
            )
            section_input = jnp.where(
                my_section == 0, fresh_rows, stored_rows + incoming.astype(jnp.float32)
            )
            row_scale, normed, pre_act, active = normalize(section_input, gain_row, down_weight)
            output = section_input + jnp.dot(active, up_weight, preferred_element_type=jnp.float32)
            previous = lax.dynamic_index_in_dim(sent_rows, slot_pick, 0, keepdims=False).astype(
                jnp.float32
            )
            change = (output - previous).astype(jnp.bfloat16)
            return (
                change,
                lax.dynamic_update_index_in_dim(stored_inputs, section_input, micro_pick, 0),
            )

        def forward_paused(unused):
            return (jnp.zeros_like(incoming), stored_inputs)

        change, stored_inputs = lax.cond(is_live, advance, forward_paused, 0)
        incoming = shifted(change, "section", 1)
        return (incoming, stored_inputs)

    start_forward = (
        jnp.zeros((row_count, feature_count), jnp.bfloat16),
        jnp.zeros((micro_count, row_count, feature_count), jnp.float32),
    )
    unused_last, stored_inputs = lax.fori_loop(0, turn_count, forward_turn, start_forward)
    start_kept = (
        jnp.zeros((feature_count, rank_count), jnp.float32),
        jnp.zeros((rank_count, feature_count), jnp.float32),
    )

    def collect(collected, normed, active, upstream_b, d_pre):
        return (
            collected[0] + over_rows(normed, d_pre),
            collected[1] + over_rows(active, upstream_b),
        )

    def backward_turn(step_now, loop_state):
        incoming, collected = loop_state
        micro_now = step_now - (section_count - 1 - my_section)
        is_live = jnp.logical_and(micro_now >= 0, micro_now < micro_count)
        micro_pick = jnp.clip(micro_now, 0, micro_count - 1)

        def retreat(unused):
            section_input = lax.dynamic_index_in_dim(stored_inputs, micro_pick, 0, keepdims=False)
            given_grad = lax.dynamic_index_in_dim(cotangent, micro_pick, 0, keepdims=False).astype(
                jnp.float32
            )
            upstream = jnp.where(
                my_section == section_count - 1, given_grad, incoming.astype(jnp.float32)
            )
            d_state, normed, active, upstream_b, d_pre = backward_layer(
                section_input, upstream, gain_row, down_weight, up_weight
            )
            return (
                d_state.astype(jnp.bfloat16),
                collect(collected, normed, active, upstream_b, d_pre),
            )

        def backward_paused(unused):
            return (jnp.zeros_like(incoming), collected)

        message, collected = lax.cond(is_live, retreat, backward_paused, 0)
        incoming = shifted(message, "section", -1)
        return (incoming, collected)

    start_backward = (jnp.zeros((row_count, feature_count), jnp.bfloat16), start_kept)
    unused_first, collected = lax.fori_loop(0, turn_count, backward_turn, start_backward)
    grad_down, grad_up = (
        lax.psum_scatter(
            collected[0].astype(jnp.bfloat16), "dp", scatter_dimension=0, tiled=True
        ).astype(jnp.float32),
        lax.psum_scatter(
            collected[1].astype(jnp.bfloat16), "dp", scatter_dimension=1, tiled=True
        ).astype(jnp.float32),
    )
    return (grad_down[None], grad_up[None])


def solution(mesh):
    placed = (
        P(None, "dp", None),
        P(None, "dp", None),
        P("dp", None),
        P("section", "dp", None, None),
        P("section", "dp", None, None),
        P("section", None),
        P("section", "dp", None),
        P("section", None, "dp"),
    )
    return jax.shard_map(
        shards,
        mesh=mesh,
        in_specs=placed,
        out_specs=(P("section", "dp", None), P("section", None, "dp")),
        check_vma=False,
    )
```

profile of v0, /device:TPU:1, one launch (start us, length us, event | category | flops | bytes accessed | tf_op | source)
XLA Modules:
  0.0 1443.7 jit_solution(8412641549927335606)
XLA Ops:
  8.7 45.3 %all-gather.3.cloned.1.call-done = bf16[1,8192,256]{2,1,0:T(8,128)(2,1)} async-done(((bf16[1,512,256]{2,1,0:T(8,128)(2,1)}), bf16[1,8192,256]{2,1,0:T(8,128)(2,1)}) %all-gather.3.cloned.1.call-update) | async-done | bytes 4194320 | tf_op jit(solution)/shard_map/all_gather | solution.py:59
  54.0 41.8 %all-gather.5.cloned.1.call-done = bf16[1,256,8192]{2,1,0:T(8,128)(2,1)} async-done(((bf16[1,256,512]{2,1,0:T(8,128)(2,1)}), bf16[1,256,8192]{2,1,0:T(8,128)(2,1)}) %all-gather.5.cloned.1.call-update) | async-done | bytes 4194320 | tf_op jit(solution)/shard_map/all_gather | solution.py:60
  98.2 383.8 %while.36 = (s32[]{:T(128)}, bf16[16,8192]{1,0:T(8,128)(2,1)S(1)}, f32[8,16,8192]{2,1,0:T(8,128)}, s32[]{:T(128)}, bf16[8,16,8192]{2,1,0:T(8,128)(2,1)S(1)}, /*i...) while((s32[]{:T(128)}, bf16[16,8192]{1,0:T(8,128)(2,1)S(1)}, ...), condition=%wide.region_4.5_spmd, body=%wide.region_0.4_spmd.sunk | while | flops 138039312 | bytes 13668444 | solution.py:108
  263.8 17.8 %collective-permute-start = (bf16[16,8192]{1,0:T(8,128)(2,1)S(1)}, bf16[16,8192]{1,0:T(8,128)(2,1)S(1)}, u32[]{:S(2)}, u32[]{:S(2)}) collective-permute-start(bf16[16,8192]{1,0:T(8,128)(2,1)S(1)} %get-tuple-element.743), channel_id=1, source_target_pairs={{0,16},{16,32},{32,48},{48,64},{64,80},{80,96},{96,112},{112,128},... | collective-permute-start | bytes 786440 | tf_op jit(solution)/shard_map/while/body/eval_jaxpr/ppermute | solution.py:12
  295.6 16.6 %collective-permute-start = (bf16[16,8192]{1,0:T(8,128)(2,1)S(1)}, bf16[16,8192]{1,0:T(8,128)(2,1)S(1)}, u32[]{:S(2)}, u32[]{:S(2)}) collective-permute-start(bf16[16,8192]{1,0:T(8,128)(2,1)S(1)} %get-tuple-element.743), channel_id=1, source_target_pairs={{0,16},{16,32},{32,48},{48,64},{64,80},{80,96},{96,112},{112,128},... | collective-permute-start | bytes 786440 | tf_op jit(solution)/shard_map/while/body/eval_jaxpr/ppermute | solution.py:12
  461.1 17.6 %collective-permute-start = (bf16[16,8192]{1,0:T(8,128)(2,1)S(1)}, bf16[16,8192]{1,0:T(8,128)(2,1)S(1)}, u32[]{:S(2)}, u32[]{:S(2)}) collective-permute-start(bf16[16,8192]{1,0:T(8,128)(2,1)S(1)} %get-tuple-element.743), channel_id=1, source_target_pairs={{0,16},{16,32},{32,48},{48,64},{64,80},{80,96},{96,112},{112,128},... | collective-permute-start | bytes 786440 | tf_op jit(solution)/shard_map/while/body/eval_jaxpr/ppermute | solution.py:12
  490.0 761.7 %while.37 = (s32[]{:T(128)}, bf16[16,8192]{1,0:T(8,128)(2,1)S(1)}, f32[8192,256]{1,0:T(8,128)}, f32[256,8192]{1,0:T(8,128)}, s32[]{:T(128)}, /*index=5*/s32[]{:T...) while((s32[]{:T(128)}, bf16[16,8192]{1,0:T(8,128)(2,1)S(1)}, ...), condition=%wide.region_10.11_spmd, body=%wide.region_5.10_spmd.sunk | while | flops 343466048 | bytes 212247904 | solution.py:150
  502.6 16.4 %collective-permute-done.1 = bf16[16,8192]{1,0:T(8,128)(2,1)S(1)} collective-permute-done((bf16[16,8192]{1,0:T(8,128)(2,1)S(1)}, bf16[16,8192]{1,0:T(8,128)(2,1)S(1)}, u32[]{:S(2)}, u32[]{:S(2)}) %collective-permute-start.1) | collective-permute-done | bytes 262176 | tf_op jit(solution)/shard_map/while/body/eval_jaxpr/ppermute | solution.py:12
  531.0 19.7 %collective-permute-done.1 = bf16[16,8192]{1,0:T(8,128)(2,1)S(1)} collective-permute-done((bf16[16,8192]{1,0:T(8,128)(2,1)S(1)}, bf16[16,8192]{1,0:T(8,128)(2,1)S(1)}, u32[]{:S(2)}, u32[]{:S(2)}) %collective-permute-start.1) | collective-permute-done | bytes 262176 | tf_op jit(solution)/shard_map/while/body/eval_jaxpr/ppermute | solution.py:12
  584.4 16.9 %collective-permute-done.1 = bf16[16,8192]{1,0:T(8,128)(2,1)S(1)} collective-permute-done((bf16[16,8192]{1,0:T(8,128)(2,1)S(1)}, bf16[16,8192]{1,0:T(8,128)(2,1)S(1)}, u32[]{:S(2)}, u32[]{:S(2)}) %collective-permute-start.1) | collective-permute-done | bytes 262176 | tf_op jit(solution)/shard_map/while/body/eval_jaxpr/ppermute | solution.py:12
  614.1 17.4 %collective-permute-done.1 = bf16[16,8192]{1,0:T(8,128)(2,1)S(1)} collective-permute-done((bf16[16,8192]{1,0:T(8,128)(2,1)S(1)}, bf16[16,8192]{1,0:T(8,128)(2,1)S(1)}, u32[]{:S(2)}, u32[]{:S(2)}) %collective-permute-start.1) | collective-permute-done | bytes 262176 | tf_op jit(solution)/shard_map/while/body/eval_jaxpr/ppermute | solution.py:12
  675.6 16.8 %collective-permute-done.1 = bf16[16,8192]{1,0:T(8,128)(2,1)S(1)} collective-permute-done((bf16[16,8192]{1,0:T(8,128)(2,1)S(1)}, bf16[16,8192]{1,0:T(8,128)(2,1)S(1)}, u32[]{:S(2)}, u32[]{:S(2)}) %collective-permute-start.1) | collective-permute-done | bytes 262176 | tf_op jit(solution)/shard_map/while/body/eval_jaxpr/ppermute | solution.py:12
  693.7 302.6 %collective-permute-done.1 = bf16[16,8192]{1,0:T(8,128)(2,1)S(1)} collective-permute-done((bf16[16,8192]{1,0:T(8,128)(2,1)S(1)}, bf16[16,8192]{1,0:T(8,128)(2,1)S(1)}, u32[]{:S(2)}, u32[]{:S(2)}) %collective-permute-start.1) | collective-permute-done | bytes 262176 | tf_op jit(solution)/shard_map/while/body/eval_jaxpr/ppermute | solution.py:12
  996.3 20.5 %conditional.5 = (bf16[16,8192]{1,0:T(8,128)(2,1)S(1)}, f32[8192,256]{1,0:T(8,128)}, f32[256,8192]{1,0:T(8,128)}) conditional(s32[]{:T(128)} %convert_element_type.146, (f32[8192,256]{1,0:T(8,128)}, f32[256,8192]{1,0:T(8,128)}) %tuple.95, (s32[]{:T(128)}, s32[]{:T(128)}, bf16[8,16,8192]{2,1,0:T(8,128)(2,1)}, bf16[16,8192]{1,0:T(8,128)(2,1)S(1)}, ...), branch_computations={%region_6.6_spmd, %region_7.9_spmd} | conditional | flops 343466048 | bytes 211199008 | solution.py:145
  1018.2 21.3 %collective-permute-done.1 = bf16[16,8192]{1,0:T(8,128)(2,1)S(1)} collective-permute-done((bf16[16,8192]{1,0:T(8,128)(2,1)S(1)}, bf16[16,8192]{1,0:T(8,128)(2,1)S(1)}, u32[]{:S(2)}, u32[]{:S(2)}) %collective-permute-start.1) | collective-permute-done | bytes 262176 | tf_op jit(solution)/shard_map/while/body/eval_jaxpr/ppermute | solution.py:12
  1039.4 20.5 %conditional.5 = (bf16[16,8192]{1,0:T(8,128)(2,1)S(1)}, f32[8192,256]{1,0:T(8,128)}, f32[256,8192]{1,0:T(8,128)}) conditional(s32[]{:T(128)} %convert_element_type.146, (f32[8192,256]{1,0:T(8,128)}, f32[256,8192]{1,0:T(8,128)}) %tuple.95, (s32[]{:T(128)}, s32[]{:T(128)}, bf16[8,16,8192]{2,1,0:T(8,128)(2,1)}, bf16[16,8192]{1,0:T(8,128)(2,1)S(1)}, ...), branch_computations={%region_6.6_spmd, %region_7.9_spmd} | conditional | flops 343466048 | bytes 211199008 | solution.py:145
  1069.9 20.6 %conditional.5 = (bf16[16,8192]{1,0:T(8,128)(2,1)S(1)}, f32[8192,256]{1,0:T(8,128)}, f32[256,8192]{1,0:T(8,128)}) conditional(s32[]{:T(128)} %convert_element_type.146, (f32[8192,256]{1,0:T(8,128)}, f32[256,8192]{1,0:T(8,128)}) %tuple.95, (s32[]{:T(128)}, s32[]{:T(128)}, bf16[8,16,8192]{2,1,0:T(8,128)(2,1)}, bf16[16,8192]{1,0:T(8,128)(2,1)S(1)}, ...), branch_computations={%region_6.6_spmd, %region_7.9_spmd} | conditional | flops 343466048 | bytes 211199008 | solution.py:145
  1100.0 20.6 %conditional.5 = (bf16[16,8192]{1,0:T(8,128)(2,1)S(1)}, f32[8192,256]{1,0:T(8,128)}, f32[256,8192]{1,0:T(8,128)}) conditional(s32[]{:T(128)} %convert_element_type.146, (f32[8192,256]{1,0:T(8,128)}, f32[256,8192]{1,0:T(8,128)}) %tuple.95, (s32[]{:T(128)}, s32[]{:T(128)}, bf16[8,16,8192]{2,1,0:T(8,128)(2,1)}, bf16[16,8192]{1,0:T(8,128)(2,1)S(1)}, ...), branch_computations={%region_6.6_spmd, %region_7.9_spmd} | conditional | flops 343466048 | bytes 211199008 | solution.py:145
  1130.0 20.5 %conditional.5 = (bf16[16,8192]{1,0:T(8,128)(2,1)S(1)}, f32[8192,256]{1,0:T(8,128)}, f32[256,8192]{1,0:T(8,128)}) conditional(s32[]{:T(128)} %convert_element_type.146, (f32[8192,256]{1,0:T(8,128)}, f32[256,8192]{1,0:T(8,128)}) %tuple.95, (s32[]{:T(128)}, s32[]{:T(128)}, bf16[8,16,8192]{2,1,0:T(8,128)(2,1)}, bf16[16,8192]{1,0:T(8,128)(2,1)S(1)}, ...), branch_computations={%region_6.6_spmd, %region_7.9_spmd} | conditional | flops 343466048 | bytes 211199008 | solution.py:145
  1160.4 20.5 %conditional.5 = (bf16[16,8192]{1,0:T(8,128)(2,1)S(1)}, f32[8192,256]{1,0:T(8,128)}, f32[256,8192]{1,0:T(8,128)}) conditional(s32[]{:T(128)} %convert_element_type.146, (f32[8192,256]{1,0:T(8,128)}, f32[256,8192]{1,0:T(8,128)}) %tuple.95, (s32[]{:T(128)}, s32[]{:T(128)}, bf16[8,16,8192]{2,1,0:T(8,128)(2,1)}, bf16[16,8192]{1,0:T(8,128)(2,1)S(1)}, ...), branch_computations={%region_6.6_spmd, %region_7.9_spmd} | conditional | flops 343466048 | bytes 211199008 | solution.py:145
  1191.3 20.5 %conditional.5 = (bf16[16,8192]{1,0:T(8,128)(2,1)S(1)}, f32[8192,256]{1,0:T(8,128)}, f32[256,8192]{1,0:T(8,128)}) conditional(s32[]{:T(128)} %convert_element_type.146, (f32[8192,256]{1,0:T(8,128)}, f32[256,8192]{1,0:T(8,128)}) %tuple.95, (s32[]{:T(128)}, s32[]{:T(128)}, bf16[8,16,8192]{2,1,0:T(8,128)(2,1)}, bf16[16,8192]{1,0:T(8,128)(2,1)S(1)}, ...), branch_computations={%region_6.6_spmd, %region_7.9_spmd} | conditional | flops 343466048 | bytes 211199008 | solution.py:145
  1222.6 20.5 %conditional.5 = (bf16[16,8192]{1,0:T(8,128)(2,1)S(1)}, f32[8192,256]{1,0:T(8,128)}, f32[256,8192]{1,0:T(8,128)}) conditional(s32[]{:T(128)} %convert_element_type.146, (f32[8192,256]{1,0:T(8,128)}, f32[256,8192]{1,0:T(8,128)}) %tuple.95, (s32[]{:T(128)}, s32[]{:T(128)}, bf16[8,16,8192]{2,1,0:T(8,128)(2,1)}, bf16[16,8192]{1,0:T(8,128)(2,1)S(1)}, ...), branch_computations={%region_6.6_spmd, %region_7.9_spmd} | conditional | flops 343466048 | bytes 211199008 | solution.py:145
  1263.4 101.6 %reduce-scatter.3.cloned.1.call-done = bf16[512,256]{1,0:T(8,128)(2,1)} async-done(((bf16[8192,256]{1,0:T(8,128)(2,1)}), bf16[512,256]{1,0:T(8,128)(2,1)}) %reduce-scatter.3.cloned.1.call-update) | async-done | bytes 262160 | tf_op jit(solution)/shard_map/reduce_scatter | solution.py:152
  1366.8 68.6 %reduce-scatter.5.cloned.1.call-done = bf16[256,512]{1,0:T(8,128)(2,1)} async-done(((bf16[256,8192]{1,0:T(8,128)(2,1)}), bf16[256,512]{1,0:T(8,128)(2,1)}) %reduce-scatter.5.cloned.1.call-update) | async-done | bytes 262160 | tf_op jit(solution)/shard_map/reduce_scatter | solution.py:155
  (405 shorter events, 786.4 us)
Async XLA Ops:
  7.2 46.8 %all-gather.3.cloned.1.call-start = ((), (), s32[]{:S(2)}) async-start(), calls=%async_computation.2 | async-start | bytes 4456448 | tf_op jit(solution)/shard_map/all_gather | solution.py:59
  7.9 87.9 %all-gather.5.cloned.1.call-start = ((), (), s32[]{:S(2)}) async-start(), calls=%async_computation.3 | async-start | bytes 4456448 | tf_op jit(solution)/shard_map/all_gather | solution.py:60
  8.7 1356.3 %reduce-scatter.3.cloned.1.call-start = ((), (), s32[]{:S(2)}) async-start(), calls=%async_computation.4 | async-start | bytes 4456448 | tf_op jit(solution)/shard_map/reduce_scatter | solution.py:152
  263.8 21.1 %collective-permute-start = (bf16[16,8192]{1,0:T(8,128)(2,1)S(1)}, bf16[16,8192]{1,0:T(8,128)(2,1)S(1)}, u32[]{:S(2)}, u32[]{:S(2)}) collective-permute-start(bf16[16,8192]{1,0:T(8,128)(2,1)S(1)} %get-tuple-element.743), channel_id=1, source_target_pairs={{0,16},{16,32},{32,48},{48,64},{64,80},{80,96},{96,112},{112,128},... | collective-permute-start | bytes 786440 | tf_op jit(solution)/shard_map/while/body/eval_jaxpr/ppermute | solution.py:12
  295.6 19.9 %collective-permute-start = (bf16[16,8192]{1,0:T(8,128)(2,1)S(1)}, bf16[16,8192]{1,0:T(8,128)(2,1)S(1)}, u32[]{:S(2)}, u32[]{:S(2)}) collective-permute-start(bf16[16,8192]{1,0:T(8,128)(2,1)S(1)} %get-tuple-element.743), channel_id=1, source_target_pairs={{0,16},{16,32},{32,48},{48,64},{64,80},{80,96},{96,112},{112,128},... | collective-permute-start | bytes 786440 | tf_op jit(solution)/shard_map/while/body/eval_jaxpr/ppermute | solution.py:12
  315.6 14.4 collective-permute-start
  330.0 13.2 collective-permute-start
  351.9 16.4 %collective-permute-start = (bf16[16,8192]{1,0:T(8,128)(2,1)S(1)}, bf16[16,8192]{1,0:T(8,128)(2,1)S(1)}, u32[]{:S(2)}, u32[]{:S(2)}) collective-permute-start(bf16[16,8192]{1,0:T(8,128)(2,1)S(1)} %get-tuple-element.743), channel_id=1, source_target_pairs={{0,16},{16,32},{32,48},{48,64},{64,80},{80,96},{96,112},{112,128},... | collective-permute-start | bytes 786440 | tf_op jit(solution)/shard_map/while/body/eval_jaxpr/ppermute | solution.py:12
  379.3 20.8 %collective-permute-start = (bf16[16,8192]{1,0:T(8,128)(2,1)S(1)}, bf16[16,8192]{1,0:T(8,128)(2,1)S(1)}, u32[]{:S(2)}, u32[]{:S(2)}) collective-permute-start(bf16[16,8192]{1,0:T(8,128)(2,1)S(1)} %get-tuple-element.743), channel_id=1, source_target_pairs={{0,16},{16,32},{32,48},{48,64},{64,80},{80,96},{96,112},{112,128},... | collective-permute-start | bytes 786440 | tf_op jit(solution)/shard_map/while/body/eval_jaxpr/ppermute | solution.py:12
  410.4 15.4 %collective-permute-start = (bf16[16,8192]{1,0:T(8,128)(2,1)S(1)}, bf16[16,8192]{1,0:T(8,128)(2,1)S(1)}, u32[]{:S(2)}, u32[]{:S(2)}) collective-permute-start(bf16[16,8192]{1,0:T(8,128)(2,1)S(1)} %get-tuple-element.743), channel_id=1, source_target_pairs={{0,16},{16,32},{32,48},{48,64},{64,80},{80,96},{96,112},{112,128},... | collective-permute-start | bytes 786440 | tf_op jit(solution)/shard_map/while/body/eval_jaxpr/ppermute | solution.py:12
  434.8 17.6 %collective-permute-start = (bf16[16,8192]{1,0:T(8,128)(2,1)S(1)}, bf16[16,8192]{1,0:T(8,128)(2,1)S(1)}, u32[]{:S(2)}, u32[]{:S(2)}) collective-permute-start(bf16[16,8192]{1,0:T(8,128)(2,1)S(1)} %get-tuple-element.743), channel_id=1, source_target_pairs={{0,16},{16,32},{32,48},{48,64},{64,80},{80,96},{96,112},{112,128},... | collective-permute-start | bytes 786440 | tf_op jit(solution)/shard_map/while/body/eval_jaxpr/ppermute | solution.py:12
  461.1 20.9 %collective-permute-start = (bf16[16,8192]{1,0:T(8,128)(2,1)S(1)}, bf16[16,8192]{1,0:T(8,128)(2,1)S(1)}, u32[]{:S(2)}, u32[]{:S(2)}) collective-permute-start(bf16[16,8192]{1,0:T(8,128)(2,1)S(1)} %get-tuple-element.743), channel_id=1, source_target_pairs={{0,16},{16,32},{32,48},{48,64},{64,80},{80,96},{96,112},{112,128},... | collective-permute-start | bytes 786440 | tf_op jit(solution)/shard_map/while/body/eval_jaxpr/ppermute | solution.py:12
  501.3 17.7 %collective-permute-start.1 = (bf16[16,8192]{1,0:T(8,128)(2,1)S(1)}, bf16[16,8192]{1,0:T(8,128)(2,1)S(1)}, u32[]{:S(2)}, u32[]{:S(2)}) collective-permute-start(bf16[16,8192]{1,0:T(8,128)(2,1)S(1)} %get-tuple-element.756), channel_id=1, source_target_pairs={{16,0},{32,16},{48,32},{64,48},{80,64},{96,80},{112,96},{128,112},... | collective-permute-start | bytes 786440 | tf_op jit(solution)/shard_map/while/body/eval_jaxpr/ppermute | solution.py:12
  529.7 21.0 %collective-permute-start.1 = (bf16[16,8192]{1,0:T(8,128)(2,1)S(1)}, bf16[16,8192]{1,0:T(8,128)(2,1)S(1)}, u32[]{:S(2)}, u32[]{:S(2)}) collective-permute-start(bf16[16,8192]{1,0:T(8,128)(2,1)S(1)} %get-tuple-element.756), channel_id=1, source_target_pairs={{16,0},{32,16},{48,32},{64,48},{80,64},{96,80},{112,96},{128,112},... | collective-permute-start | bytes 786440 | tf_op jit(solution)/shard_map/while/body/eval_jaxpr/ppermute | solution.py:12
  571.6 11.5 collective-permute-start.1
  583.1 18.2 %collective-permute-start.1 = (bf16[16,8192]{1,0:T(8,128)(2,1)S(1)}, bf16[16,8192]{1,0:T(8,128)(2,1)S(1)}, u32[]{:S(2)}, u32[]{:S(2)}) collective-permute-start(bf16[16,8192]{1,0:T(8,128)(2,1)S(1)} %get-tuple-element.756), channel_id=1, source_target_pairs={{16,0},{32,16},{48,32},{64,48},{80,64},{96,80},{112,96},{128,112},... | collective-permute-start | bytes 786440 | tf_op jit(solution)/shard_map/while/body/eval_jaxpr/ppermute | solution.py:12
  612.8 18.7 %collective-permute-start.1 = (bf16[16,8192]{1,0:T(8,128)(2,1)S(1)}, bf16[16,8192]{1,0:T(8,128)(2,1)S(1)}, u32[]{:S(2)}, u32[]{:S(2)}) collective-permute-start(bf16[16,8192]{1,0:T(8,128)(2,1)S(1)} %get-tuple-element.756), channel_id=1, source_target_pairs={{16,0},{32,16},{48,32},{64,48},{80,64},{96,80},{112,96},{128,112},... | collective-permute-start | bytes 786440 | tf_op jit(solution)/shard_map/while/body/eval_jaxpr/ppermute | solution.py:12
  631.5 13.5 collective-permute-start.1
  645.1 15.1 %collective-permute-start.1 = (bf16[16,8192]{1,0:T(8,128)(2,1)S(1)}, bf16[16,8192]{1,0:T(8,128)(2,1)S(1)}, u32[]{:S(2)}, u32[]{:S(2)}) collective-permute-start(bf16[16,8192]{1,0:T(8,128)(2,1)S(1)} %get-tuple-element.756), channel_id=1, source_target_pairs={{16,0},{32,16},{48,32},{64,48},{80,64},{96,80},{112,96},{128,112},... | collective-permute-start | bytes 786440 | tf_op jit(solution)/shard_map/while/body/eval_jaxpr/ppermute | solution.py:12
  660.2 14.0 collective-permute-start.1
  674.3 18.1 %collective-permute-start.1 = (bf16[16,8192]{1,0:T(8,128)(2,1)S(1)}, bf16[16,8192]{1,0:T(8,128)(2,1)S(1)}, u32[]{:S(2)}, u32[]{:S(2)}) collective-permute-start(bf16[16,8192]{1,0:T(8,128)(2,1)S(1)} %get-tuple-element.756), channel_id=1, source_target_pairs={{16,0},{32,16},{48,32},{64,48},{80,64},{96,80},{112,96},{128,112},... | collective-permute-start | bytes 786440 | tf_op jit(solution)/shard_map/while/body/eval_jaxpr/ppermute | solution.py:12
  692.4 303.9 %collective-permute-start.1 = (bf16[16,8192]{1,0:T(8,128)(2,1)S(1)}, bf16[16,8192]{1,0:T(8,128)(2,1)S(1)}, u32[]{:S(2)}, u32[]{:S(2)}) collective-permute-start(bf16[16,8192]{1,0:T(8,128)(2,1)S(1)} %get-tuple-element.756), channel_id=1, source_target_pairs={{16,0},{32,16},{48,32},{64,48},{80,64},{96,80},{112,96},{128,112},... | collective-permute-start | bytes 786440 | tf_op jit(solution)/shard_map/while/body/eval_jaxpr/ppermute | solution.py:12
  1016.9 22.6 %collective-permute-start.1 = (bf16[16,8192]{1,0:T(8,128)(2,1)S(1)}, bf16[16,8192]{1,0:T(8,128)(2,1)S(1)}, u32[]{:S(2)}, u32[]{:S(2)}) collective-permute-start(bf16[16,8192]{1,0:T(8,128)(2,1)S(1)} %get-tuple-element.756), channel_id=1, source_target_pairs={{16,0},{32,16},{48,32},{64,48},{80,64},{96,80},{112,96},{128,112},... | collective-permute-start | bytes 786440 | tf_op jit(solution)/shard_map/while/body/eval_jaxpr/ppermute | solution.py:12
  1257.5 178.0 %reduce-scatter.5.cloned.1.call-start = ((), (), s32[]{:S(2)}) async-start(), calls=%async_computation.5 | async-start | bytes 4456448 | tf_op jit(solution)/shard_map/reduce_scatter | solution.py:155
  (85 other events, 771.3 us)
Sparse Core Ops, SparseCore 0:
  9.9 44.0 all-gather.2
  55.8 39.9 all-gather.4
  1257.6 107.3 reduce-scatter.2
  1367.4 67.9 reduce-scatter.4
where the time goes:
time: 1450 us; the launch traced here: 1440 us
  waiting for transfers between devices  920 us (63%)
  starting transfers between devices  226 us (16%)
  matrix products  161 us (11%)
  other arithmetic  62.3 us (4%)
  local copies, waits for them, and re-layouts  44.1 us (3%)
  loops' own time  17.1 us (1%)
    ppermute x46, waiting for transfers between devices, shifted(): lax.ppermute(value, axis, [(source, source + steps) for source in range(l...  661 us
    ppermute x46, starting transfers between devices, shifted(): lax.ppermute(value, axis, [(source, source + steps) for source in range(l...  225 us
    reduce_scatter x1, waiting for transfers between devices, shards(): lax.psum_scatter(collected[0].astype(jnp.bfloat16), 'dp', scatter_dimensi...  102 us
    reduce_scatter x1, waiting for transfers between devices, shards(): lax.psum_scatter(collected[1].astype(jnp.bfloat16), 'dp', scatter_dimensi...  68.6 us
    dot_general x16, matrix products, over_rows(): lax.dot_general(operand_a, operand_b, (((0,), (0,)), ((), ())), preferred...  48.9 us
    dot_general x8, matrix products, advance(): jnp.dot(active, up_weight, preferred_element_type=jnp.float32)  48.4 us
    all_gather x1, waiting for transfers between devices, shards(): lax.all_gather(down_proj, 'dp', axis=1, tiled=True)  45.3 us
    all_gather x1, waiting for transfers between devices, shards(): lax.all_gather(up_proj, 'dp', axis=2, tiled=True)  41.8 us
  transfers between devices with their start and end apart: 50, of which 50 were waited for; matrix products, arithmetic and copies ran while one was open for 1% of the time, Pallas kernels for 0%

commit v1 on v0

v1 whole, which is shorter than its diff:
```python
import functools

import jax
import jax.numpy as jnp
from jax import lax
from jax.experimental import pallas as pl
from jax.experimental.pallas import tpu as pltpu
from jax.sharding import PartitionSpec as P

MESH = pl.DeviceIdType.MESH
F32, BF16 = jnp.float32, jnp.bfloat16
EPS = 1e-05
D = 8192
HALF = 4096
RANK = 256
TOK = 16
MB = 8
CH = 512
COLS = 1024
NCOL = HALF // COLS
STAGES = 8


def nt(a, b):
    return lax.dot_general(a, b, (((1,), (1,)), ((), ())), preferred_element_type=F32)


def tn(a, b):
    return lax.dot_general(a, b, (((0,), (0,)), ((), ())), preferred_element_type=F32)


def nn(a, b):
    return jnp.dot(a, b, preferred_element_type=F32)


def lanes(v):
    total = v[:, 0:128]
    for k in range(128, v.shape[1], 128):
        total = total + v[:, k : k + 128]
    return total


def kernel(
    rec_in, sent_in, down_in, up_in, gd_out, gu_out,
    rec, sent, wd, wu, xin, uin, xs, um, xf, fout, bout, red_tx, red_rx,
    pre, act, vee, scl, gds, gus, gdl, gul,
    s_tab, r_tab, s_w, r_w, s_hf, r_hf, s_hb, r_hb, s_red, r_red, s_g, r_g,
):
    s = lax.axis_index("section")
    e = lax.axis_index("dp")
    h, z = lax.rem(s, 2), lax.div(s, 2)
    c, q = lax.rem(e, 2), lax.div(e, 2)
    chip = h * 8 + q
    owner_core = lax.div(e, 8)
    local = c == owner_core
    other = (s, e + 1 - 2 * c)

    barrier = pltpu.get_barrier_semaphore()

    def greet(t, carry):
        place = lax.rem(h * 16 + e + t, 32)
        pl.semaphore_signal(
            barrier, inc=1, device_id=(2 * z + lax.div(place, 16), lax.rem(place, 16)), device_id_type=MESH
        )
        return carry

    lax.fori_loop(1, 32, greet, 0)

    @pl.when(z > 0)
    def _():
        pl.semaphore_signal(barrier, inc=1, device_id=(s - 2, e), device_id_type=MESH)

    @pl.when(z < STAGES - 1)
    def _():
        pl.semaphore_signal(barrier, inc=1, device_id=(s + 2, e), device_id_type=MESH)

    neighbours = jnp.where(z > 0, 1, 0) + jnp.where(z < STAGES - 1, 1, 0)
    pl.semaphore_wait(barrier, 31 + neighbours)

    def table_copy(which, k, t):
        src = (rec_in, sent_in)[which]
        dst = (rec, sent)[which]
        h2, c2 = lax.rem(h + t // 2, 2), lax.rem(c + t, 2)
        row = pl.multiple_of((2 * k + c) * TOK, TOK)
        return dict(
            src_ref=src.at[4 * h2 + k, :, pl.ds(pl.multiple_of(c2 * HALF, HALF), HALF)],
            dst_ref=dst.at[h, pl.ds(row, TOK), :],
        ), s_tab.at[which, k, t], r_tab.at[which, h, 2 * k + c], (2 * z + h2, 2 * q + c2)

    def table_start(which, k):
        for t in range(4):
            refs, ssem, rsem, dev = table_copy(which, k, t)
            if t == 0:
                pltpu.make_async_copy(refs["src_ref"], refs["dst_ref"], rsem).start()
            else:
                pltpu.make_async_remote_copy(
                    **refs, send_sem=ssem, recv_sem=rsem, device_id=dev, device_id_type=MESH
                ).start()

    def table_sent(which, k):
        for t in range(1, 4):
            refs, ssem, rsem, dev = table_copy(which, k, t)
            pltpu.make_async_remote_copy(
                **refs, send_sem=ssem, recv_sem=rsem, device_id=dev, device_id_type=MESH
            ).wait_send()

    def table_wait(which, part, i):
        place = (rec, sent)[which].at[part, pl.ds(pl.multiple_of(i * TOK, TOK), TOK), :]
        pltpu.make_async_copy(place, place, r_tab.at[which, part, i]).wait()

    slot = lax.rem(e, 8)
    spot = pl.multiple_of(slot * CH, CH)

    def weight_refs(kind):
        if kind == 0:
            return down_in, wd.at[h, pl.ds(spot, CH), :]
        return up_in, wu.at[h, :, pl.ds(spot, CH)]

    def weight_remote(kind, t):
        src, dst = weight_refs(kind)
        place = lax.rem(chip + t, 16)
        return pltpu.make_async_remote_copy(
            src_ref=src, dst_ref=dst, send_sem=s_w.at[kind, t], recv_sem=r_w.at[kind, h, slot],
            device_id=(2 * z + lax.div(place, 8), 2 * lax.rem(place, 8) + owner_core), device_id_type=MESH,
        )

    def weight_start(kind):
        @pl.when(local)
        def _():
            src, dst = weight_refs(kind)
            pltpu.make_async_copy(src, dst, r_w.at[kind, h, slot]).start()

        @pl.when(jnp.logical_not(local))
        def _():
            weight_remote(kind, 0).start()

        def more(t, carry):
            weight_remote(kind, t).start()
            return carry

        lax.fori_loop(1, 16, more, 0)

    def weight_sent(kind):
        @pl.when(jnp.logical_not(local))
        def _():
            weight_remote(kind, 0).wait_send()

        def more(t, carry):
            weight_remote(kind, t).wait_send()
            return carry

        lax.fori_loop(1, 16, more, 0)

    def weight_wait(kind, part):
        def one(j, carry):
            at = pl.ds(pl.multiple_of(j * CH, CH), CH)
            place = wd.at[part, at, :] if kind == 0 else wu.at[part, :, at]
            pltpu.make_async_copy(place, place, r_w.at[kind, part, j]).wait()
            return carry

        lax.fori_loop(0, 8, one, 0)

    table_start(0, 0)
    weight_start(0)
    weight_start(1)
    table_start(1, 0)
    for k in range(1, 4):
        table_start(0, k)
        table_start(1, k)

    def red_copy(n):
        return pltpu.make_async_remote_copy(
            src_ref=red_tx.at[n], dst_ref=red_rx.at[n], send_sem=s_red.at[n], recv_sem=r_red.at[n],
            device_id=other, device_id_type=MESH,
        )

    def col(n):
        return slice(n * COLS, (n + 1) * COLS)

    def hop(n, i, ahead):
        at = (slice(None), col(n))
        if ahead:
            buf, dst, ss, rs, dev = fout, xin, s_hf, r_hf, (s + 2, e)
        else:
            buf, dst, ss, rs, dev = bout, uin, s_hb, r_hb, (s - 2, e)
        rows = pl.ds(pl.multiple_of(i * TOK, TOK), TOK)
        return pltpu.make_async_remote_copy(
            src_ref=buf.at[rows, col(n)], dst_ref=dst.at[rows, col(n)], send_sem=ss.at[i, n], recv_sem=rs.at[i, n],
            device_id=dev, device_id_type=MESH,
        )

    def forward(i, carry):
        rows = pl.ds(pl.multiple_of(i * TOK, TOK), TOK)
        table_wait(0, 0, i)

        @pl.when(i == 0)
        def _():
            weight_wait(0, 0)

        acc = jnp.zeros((TOK, RANK), F32)
        sq = jnp.zeros((TOK, 128), F32)
        for n in range(NCOL):
            @pl.when(z > 0)
            def _():
                hop(n, i, True).wait_recv()
                xf[:, col(n)] = rec[0, rows, col(n)].astype(F32) + xin[rows, col(n)].astype(F32)

            @pl.when(z == 0)
            def _():
                xf[:, col(n)] = rec[0, rows, col(n)].astype(F32)

            x = xf[:, col(n)]
            xb = x.astype(BF16)
            xs[0, rows, col(n)] = xb
            sq = sq + lanes(x * x)
            acc = acc + nn(xb, wd[0, col(n), :])

        def finish(part, acc, sq):
            n = 2 * i + part
            red_tx[n, :, 0:RANK] = acc
            red_tx[n, :, RANK:] = sq
            red_copy(n).start()
            red_copy(n).wait_recv()
            total = acc + red_rx[n, :, 0:RANK]
            square = jnp.sum(sq + red_rx[n, :, RANK:], axis=1, keepdims=True)
            scale = lax.rsqrt(square * (1.0 / D) + EPS)
            v = total * scale
            pre[part, rows, :] = v
            scl[part, rows, :] = jnp.broadcast_to(scale, (TOK, 128))
            a = (v * jax.nn.sigmoid(v)).astype(BF16)
            act[part, rows, :] = a
            return a

        a = finish(0, acc, sq)

        @pl.when(i == 0)
        def _():
            weight_wait(1, 0)
            weight_wait(0, 1)

        table_wait(0, 1, i)
        table_wait(1, 0, i)
        acc = jnp.zeros((TOK, RANK), F32)
        sq = jnp.zeros((TOK, 128), F32)
        for n in range(NCOL):
            x = (
                xf[:, col(n)] + nn(a, wu[0, :, col(n)])
                + (rec[1, rows, col(n)].astype(F32) - sent[0, rows, col(n)].astype(F32))
            )
            xf[:, col(n)] = x
            xb = x.astype(BF16)
            xs[1, rows, col(n)] = xb
            sq = sq + lanes(x * x)
            acc = acc + nn(xb, wd[1, col(n), :])
        a = finish(1, acc, sq)

        @pl.when(i == 0)
        def _():
            weight_wait(1, 1)

        table_wait(1, 1, i)

        @pl.when(z < STAGES - 1)
        def _():
            for n in range(NCOL):
                x = xf[:, col(n)] + nn(a, wu[1, :, col(n)]) - sent[1, rows, col(n)].astype(F32)
                fout[rows, col(n)] = x.astype(BF16)
                hop(n, i, True).start()

        return carry

    lax.fori_loop(0, MB, forward, 0)

    def backward(i, carry):
        rows = pl.ds(pl.multiple_of(i * TOK, TOK), TOK)
        acc = jnp.zeros((TOK, RANK), F32)
        for n in range(NCOL):
            @pl.when(z < STAGES - 1)
            def _():
                hop(n, i, False).wait_recv()

            @pl.when(z == STAGES - 1)
            def _():
                uin[rows, col(n)] = sent[1, rows, col(n)]

            acc = acc + nt(uin[rows, col(n)], wu[1, :, col(n)])

        def finish(part, acc):
            n = 2 * MB + 2 * i + part
            red_tx[n, :, 0:RANK] = acc
            red_tx[n, :, RANK:] = jnp.zeros((TOK, 128), F32)
            red_copy(n).start()
            red_copy(n).wait_recv()
            total = acc + red_rx[n, :, 0:RANK]
            v = pre[part, rows, :]
            gate = jax.nn.sigmoid(v)
            d_pre = total * gate * (1.0 + v * (1.0 - gate))
            scale = scl[part, rows, 0:1]
            mean = jnp.sum(d_pre * v, axis=1, keepdims=True) * (1.0 / D)
            back = (d_pre * scale).astype(BF16)
            vee[part, rows, :] = back
            return back, mean * scale * scale

        back, shrink = finish(1, acc)
        acc = jnp.zeros((TOK, RANK), F32)
        for n in range(NCOL):
            u = (
                uin[rows, col(n)].astype(F32) + nt(back, wd[1, col(n), :])
                - shrink * xs[1, rows, col(n)].astype(F32)
            ).astype(BF16)
            um[rows, col(n)] = u
            acc = acc + nt(u, wu[0, :, col(n)])
        back, shrink = finish(0, acc)

        @pl.when(z > 0)
        def _():
            for n in range(NCOL):
                u = (
                    um[rows, col(n)].astype(F32) + nt(back, wd[0, col(n), :])
                    - shrink * xs[0, rows, col(n)].astype(F32)
                )
                bout[rows, col(n)] = u.astype(BF16)
                hop(n, i, False).start()

        return carry

    lax.fori_loop(0, MB, backward, 0)

    def grad_copies(t):
        place = lax.rem(chip + t, 16)
        dev = (2 * z + lax.div(place, 8), 8 * c + lax.rem(place, 8))
        return [
            pltpu.make_async_remote_copy(
                src_ref=src.at[t], dst_ref=dst.at[chip], send_sem=s_g.at[kind, t], recv_sem=r_g.at[kind, chip],
                device_id=dev, device_id_type=MESH,
            )
            for kind, src, dst in ((0, gds, gdl), (1, gus, gul))
        ]

    def is_me(t):
        place = lax.rem(chip + t, 16)
        return jnp.logical_and(lax.div(place, 8) == h, 8 * c + lax.rem(place, 8) == e)

    def grads(t, carry):
        place = lax.rem(chip + t, 16)
        part, at = lax.div(place, 8), pl.ds(pl.multiple_of(lax.rem(place, 8) * CH, CH), CH)
        gds[t] = tn(xs[part, :, at], vee[part, :, :]).astype(BF16)

        @pl.when(part == 0)
        def _():
            gus[t] = tn(act[0], um[:, at]).astype(BF16)

        @pl.when(part == 1)
        def _():
            gus[t] = tn(act[1], uin[:, at]).astype(BF16)

        @pl.when(is_me(t))
        def _():
            gdl[chip] = gds[t]
            gul[chip] = gus[t]

        @pl.when(jnp.logical_not(is_me(t)))
        def _():
            for copy in grad_copies(t):
                copy.start()

        return carry

    lax.fori_loop(0, 16, grads, 0)

    gd_out[...] = jnp.zeros_like(gd_out)
    gu_out[...] = jnp.zeros_like(gu_out)

    def gather(t, carry):
        place = lax.rem(chip + 16 - t, 16)

        @pl.when(jnp.logical_not(jnp.logical_and(local, t == 0)))
        def _():
            for kind, dst in ((0, gdl), (1, gul)):
                ref = dst.at[place]
                pltpu.make_async_copy(ref, ref, r_g.at[kind, place]).wait()

        gd_out[...] += gdl[place].astype(F32)
        gu_out[...] += gul[place].astype(F32)
        return carry

    lax.fori_loop(0, 16, gather, 0)

    def grads_sent(t, carry):
        @pl.when(jnp.logical_not(is_me(t)))
        def _():
            for copy in grad_copies(t):
                copy.wait_send()

        return carry

    lax.fori_loop(0, 16, grads_sent, 0)
    weight_sent(0)
    weight_sent(1)
    for k in range(4):
        table_sent(0, k)
        table_sent(1, k)

    def rest(i, carry):
        for n in range(NCOL):
            @pl.when(z < STAGES - 1)
            def _():
                hop(n, i, True).wait_send()

            @pl.when(z > 0)
            def _():
                hop(n, i, False).wait_send()

        for k in range(4):
            red_copy(4 * i + k).wait_send()
        return carry

    lax.fori_loop(0, MB, rest, 0)


def shards(tokens, cotangent, sample_ids, sent_before, received_before, norm_gain, down_proj, up_proj):
    s = lax.axis_index("section")
    e = lax.axis_index("dp")
    last = lax.axis_size("section") - 1
    ids = sample_ids[0]
    micro = jnp.arange(MB, dtype=jnp.int32)
    where_is = jnp.sum(jnp.where(ids[None, :] == micro[:, None], micro[None, :], 0), axis=1)
    rec = jnp.where(s == 0, jnp.take(tokens, where_is, axis=0, mode="clip"), received_before[0])
    sent = jnp.where(s == last, jnp.take(cotangent, where_is, axis=0, mode="clip"), sent_before[0])
    gain = lax.dynamic_slice(norm_gain[0], (e * CH,), (CH,))[:, None]
    down = (down_proj[0].astype(F32) * gain).astype(BF16)
    any_ = pl.BlockSpec(memory_space=pl.ANY)
    vmem = pl.BlockSpec(memory_space=pltpu.VMEM)
    dma = pltpu.SemaphoreType.DMA
    rows = MB * TOK
    grad_down, grad_up = pl.pallas_call(
        kernel,
        out_shape=(jax.ShapeDtypeStruct((CH, RANK), F32), jax.ShapeDtypeStruct((RANK, CH), F32)),
        in_specs=[any_] * 4,
        out_specs=(vmem, vmem),
        scratch_shapes=[
            pltpu.VMEM((2, rows, HALF), BF16),
            pltpu.VMEM((2, rows, HALF), BF16),
            pltpu.VMEM((2, HALF, RANK), BF16),
            pltpu.VMEM((2, RANK, HALF), BF16),
            pltpu.VMEM((rows, HALF), BF16),
            pltpu.VMEM((rows, HALF), BF16),
            pltpu.VMEM((2, rows, HALF), BF16),
            pltpu.VMEM((rows, HALF), BF16),
            pltpu.VMEM((TOK, HALF), F32),
            pltpu.VMEM((rows, HALF), BF16),
            pltpu.VMEM((rows, HALF), BF16),
            pltpu.VMEM((4 * MB, TOK, RANK + 128), F32),
            pltpu.VMEM((4 * MB, TOK, RANK + 128), F32),
            pltpu.VMEM((2, rows, RANK), F32),
            pltpu.VMEM((2, rows, RANK), BF16),
            pltpu.VMEM((2, rows, RANK), BF16),
            pltpu.VMEM((2, rows, 128), F32),
            pltpu.VMEM((16, CH, RANK), BF16),
            pltpu.VMEM((16, RANK, CH), BF16),
            pltpu.VMEM((16, CH, RANK), BF16),
            pltpu.VMEM((16, RANK, CH), BF16),
            dma((2, 4, 4)), dma((2, 2, MB)),
            dma((2, 16)), dma((2, 2, 8)),
            dma((MB, NCOL)), dma((MB, NCOL)),
            dma((MB, NCOL)), dma((MB, NCOL)),
            dma((4 * MB,)), dma((4 * MB,)),
            dma((2, 16)), dma((2, 16)),
        ],
        compiler_params=pltpu.CompilerParams(
            collective_id=0, has_side_effects=True, vmem_limit_bytes=56 * 1024 * 1024
        ),
    )(rec, sent, down, up_proj[0])
    return ((grad_down * gain)[None], grad_up[None])


def solution(mesh):
    placed = (
        P(None, "dp", None),
        P(None, "dp", None),
        P("dp", None),
        P("section", "dp", None, None),
        P("section", "dp", None, None),
        P("section", None),
        P("section", "dp", None),
        P("section", None, "dp"),
    )
    return jax.shard_map(
        shards,
        mesh=mesh,
        in_specs=placed,
        out_specs=(P("section", "dp", None), P("section", None, "dp")),
        check_vma=False,
    )
```

time: 1450 us -> 485 us (0.33)
  waiting for transfers between devices: 920 us -> 0 us
  Pallas kernels: 0 us -> 463 us
  starting transfers between devices: 226 us -> 0 us
  matrix products: 161 us -> 0 us
  other arithmetic: 62.3 us -> 9.92 us
  local copies, waits for them, and re-layouts: 44.1 us -> 8.16 us
  loops' own time: 17.1 us -> 0 us
    ppermute x46 -> x0, waiting for transfers between devices: 661 us -> none  [shifted(): lax.ppermute(value, axis, [(source, source + steps) for source in range(l...]
    pallas_call x0 -> x1, Pallas kernels: none -> 463 us  [shards(): pl.pallas_call(kernel, out_shape=(jax.ShapeDtypeStruct((CH, RANK), F32),...]
    ppermute x46 -> x0, starting transfers between devices: 225 us -> none  [shifted(): lax.ppermute(value, axis, [(source, source + steps) for source in range(l...]
    reduce_scatter x2 -> x0, waiting for transfers between devices: 170 us -> none  [the longest x1 102 us: shards(): lax.psum_scatter(collected[0].astype(jnp.bfloat16), 'dp', scatter_dimensi...]
    dot_general x48 -> x0, matrix products: 161 us -> none  [the longest x16 48.9 us: over_rows(): lax.dot_general(operand_a, operand_b, (((0,), (0,)), ((), ())), preferred...]
    all_gather x2 -> x0, waiting for transfers between devices: 87.1 us -> none  [the longest x1 45.3 us: shards(): lax.all_gather(down_proj, 'dp', axis=1, tiled=True)]
    cond x112 -> x0, local copies, waits for them, and re-layouts: 27.9 us -> none
    convert_element_type x10 -> x1, other arithmetic: 23.3 us -> 1.79 us  [shards(): down = (down_proj[0].astype(F32) * gain).astype(BF16)]
  transfers between devices with their start and end apart: 50 -> 0, of which waited for: 50 -> 0; matrix products, arithmetic and copies ran while one was open for 1% -> 0% of each run, Pallas kernels for 0% -> 0%
where the time goes in v1:
time: 485 us; the launch traced here: 482 us
  Pallas kernels  463 us (95%)
  other arithmetic  9.92 us (2%)
  local copies, waits for them, and re-layouts  8.16 us (2%)
    pallas_call x1, Pallas kernels, shards(): pl.pallas_call(kernel, out_shape=(jax.ShapeDtypeStruct((CH, RANK), F32),...  463 us

profile of v1, /device:TPU:1, one launch (start us, length us, event | category | flops | bytes accessed | tf_op | source)
XLA Modules:
  0.0 482.1 jit_solution(6385976494464652775)
XLA Ops:
  0.6 0.0 copy-start
  0.7 0.9 select_reduce_fusion
  1.6 0.7 constant_dynamic-slice_fusion
  2.3 1.8 fusion.down_in
  4.0 0.0 copy-done
  4.1 2.0 gather_fusion.1
  6.0 3.6 gather_fusion
  9.7 5.2 %bitcast_select_fusion = (bf16[8,16,8192]{2,1,0:T(8,128)(2,1)}, bf16[8,16,8192]{2,1,0:T(8,128)(2,1)}) fusion(bf16[8,16,8192]{2,1,0:T(8,128)(2,1)} %gather_fusion.1, bf16[1,8,16,8192]{3,2,1,0:T(8,128)(2,1)} %param.11, pred[]{:T(512)S(6)} %eq.26, bf16[8,16,8192]{2,1,0:T(8,128)(2,1)} %gather_fusion, bf16[1,8,16,8192]{3,2,1,0:T(8,128)(2,1)} %param.12, pred[]{:T(512)S(6)} %eq.21), kind=kLoop, calls=%fused_computation.2 | loop fusion | flops 2097152 | bytes 12582914 | tf_op jit(solution)/shard_map/jit(_where)/select_n | solution.py:429
  14.9 463.4 %shard_map.95 = (f32[512,256]{1,0:T(8,128)}, f32[256,512]{1,0:T(8,128)}) custom-call(bf16[8,16,8192]{2,1,0:T(8,128)(2,1)} %get-tuple-element.7.rec_in, bf16[8,16,8192]{2,1,0:T(8,128)(2,1)} %get-tuple-element.6.sent_in, bf16[512,256]{1,0:T(8,128)(2,1)} %fusion.down_in, bf16[256,512]{1,0:T(8,128)(2,1)} %bitcast.14), custom_call_target="tpu_custom_call" | custom-call | tf_op jit(solution)/shard_map/pallas_call | solution.py:436
  478.3 2.0 multiply_bitcast_fusion
  480.2 1.9 copy.11
  (1 shorter events, 0.0 us)
Async XLA Ops:
  0.6 3.4 copy-start

commit v2 on v1

--- a/solution.py
+++ b/solution.py
@@ -19,6 +19,8 @@
 COLS = 1024
 NCOL = HALF // COLS
 STAGES = 8
+BATCHES = 2
+BROWS = MB * TOK // BATCHES
 
 
 def nt(a, b):
@@ -41,10 +43,10 @@
 
 
 def kernel(
-    rec_in, sent_in, down_in, up_in, gd_out, gu_out,
+    rec_in, sent_in, tok_in, cot_in, down_in, up_in, gd_out, gu_out,
     rec, sent, wd, wu, xin, uin, xs, um, xf, fout, bout, red_tx, red_rx,
-    pre, act, vee, scl, gds, gus, gdl, gul,
-    s_tab, r_tab, s_w, r_w, s_hf, r_hf, s_hb, r_hb, s_red, r_red, s_g, r_g,
+    pre, act, vee, scl, gx, ga, gv, gw,
+    s_tab, r_tab, s_w, r_w, s_x, r_x, s_hf, r_hf, s_hb, r_hb, s_red, r_red, s_g, r_g,
 ):
     s = lax.axis_index("section")
     e = lax.axis_index("dp")
@@ -77,8 +79,8 @@
     neighbours = jnp.where(z > 0, 1, 0) + jnp.where(z < STAGES - 1, 1, 0)
     pl.semaphore_wait(barrier, 31 + neighbours)
 
-    def table_copy(which, k, t):
-        src = (rec_in, sent_in)[which]
+    def table_copy(which, k, t, first=False):
+        src = ((rec_in, sent_in), (tok_in, cot_in))[first][which]
         dst = (rec, sent)[which]
         h2, c2 = lax.rem(h + t // 2, 2), lax.rem(c + t, 2)
         row = pl.multiple_of((2 * k + c) * TOK, TOK)
@@ -88,14 +90,25 @@
         ), s_tab.at[which, k, t], r_tab.at[which, h, 2 * k + c], (2 * z + h2, 2 * q + c2)
 
     def table_start(which, k):
-        for t in range(4):
-            refs, ssem, rsem, dev = table_copy(which, k, t)
-            if t == 0:
-                pltpu.make_async_copy(refs["src_ref"], refs["dst_ref"], rsem).start()
-            else:
-                pltpu.make_async_remote_copy(
-                    **refs, send_sem=ssem, recv_sem=rsem, device_id=dev, device_id_type=MESH
-                ).start()
+        end = s == (0, 2 * STAGES - 1)[which]
+
+        def start(first):
+            for t in range(4):
+                refs, ssem, rsem, dev = table_copy(which, k, t, first)
+                if t == 0:
+                    pltpu.make_async_copy(refs["src_ref"], refs["dst_ref"], rsem).start()
+                else:
+                    pltpu.make_async_remote_copy(
+                        **refs, send_sem=ssem, recv_sem=rsem, device_id=dev, device_id_type=MESH
+                    ).start()
+
+        @pl.when(end)
+        def _():
+            start(True)
+
+        @pl.when(jnp.logical_not(end))
+        def _():
+            start(False)
 
     def table_sent(which, k):
         for t in range(1, 4):
@@ -110,60 +123,83 @@
 
     slot = lax.rem(e, 8)
     spot = pl.multiple_of(slot * CH, CH)
-
-    def weight_refs(kind):
+    col_x = lax.rem(q, 4)
+    wide = pl.ds(pl.multiple_of(col_x * 2 * CH, 2 * CH), 2 * CH)
+
+    def shard_refs(kind):
         if kind == 0:
             return down_in, wd.at[h, pl.ds(spot, CH), :]
         return up_in, wu.at[h, :, pl.ds(spot, CH)]
 
-    def weight_remote(kind, t):
-        src, dst = weight_refs(kind)
-        place = lax.rem(chip + t, 16)
+    def shard_remote(kind, t):
+        src, dst = shard_refs(kind)
+        y = lax.rem(2 * h + owner_core + t, 4)
         return pltpu.make_async_remote_copy(
-            src_ref=src, dst_ref=dst, send_sem=s_w.at[kind, t], recv_sem=r_w.at[kind, h, slot],
-            device_id=(2 * z + lax.div(place, 8), 2 * lax.rem(place, 8) + owner_core), device_id_type=MESH,
+            src_ref=src, dst_ref=dst, send_sem=s_w.at[kind, t], recv_sem=r_w.at[kind, h, lax.rem(e, 2)],
+            device_id=(2 * z + lax.div(y, 2), 8 * lax.rem(y, 2) + 2 * col_x + owner_core), device_id_type=MESH,
         )
 
-    def weight_start(kind):
+    def shard_start(kind):
         @pl.when(local)
         def _():
-            src, dst = weight_refs(kind)
-            pltpu.make_async_copy(src, dst, r_w.at[kind, h, slot]).start()
+            src, dst = shard_refs(kind)
+            pltpu.make_async_copy(src, dst, r_w.at[kind, h, lax.rem(e, 2)]).start()
 
         @pl.when(jnp.logical_not(local))
         def _():
-            weight_remote(kind, 0).start()
-
-        def more(t, carry):
-            weight_remote(kind, t).start()
-            return carry
-
-        lax.fori_loop(1, 16, more, 0)
-
-    def weight_sent(kind):
+            shard_remote(kind, 0).start()
+
+        for t in range(1, 4):
+            shard_remote(kind, t).start()
+
+    def shard_sent(kind):
         @pl.when(jnp.logical_not(local))
         def _():
-            weight_remote(kind, 0).wait_send()
-
-        def more(t, carry):
-            weight_remote(kind, t).wait_send()
-            return carry
-
-        lax.fori_loop(1, 16, more, 0)
-
-    def weight_wait(kind, part):
-        def one(j, carry):
-            at = pl.ds(pl.multiple_of(j * CH, CH), CH)
+            shard_remote(kind, 0).wait_send()
+
+        for t in range(1, 4):
+            shard_remote(kind, t).wait_send()
+
+    def shard_wait(kind, part):
+        for j in range(2):
+            at = pl.ds(pl.multiple_of((2 * col_x + j) * CH, CH), CH)
             place = wd.at[part, at, :] if kind == 0 else wu.at[part, :, at]
             pltpu.make_async_copy(place, place, r_w.at[kind, part, j]).wait()
-            return carry
-
-        lax.fori_loop(0, 8, one, 0)
-
+
+    def block(kind, part, at):
+        return wd.at[part, at, :] if kind == 0 else wu.at[part, :, at]
+
+    def block_copy(kind, part, t):
+        place = block(kind, part, wide)
+        return pltpu.make_async_remote_copy(
+            src_ref=place, dst_ref=place, send_sem=s_x.at[kind, part, t], recv_sem=r_x.at[kind, part, col_x],
+            device_id=(s, e - 2 * col_x + 2 * lax.rem(col_x + t, 4)), device_id_type=MESH,
+        )
+
+    def block_start(kind, part):
+        shard_wait(kind, part)
+        for t in (1, 3, 2):
+            block_copy(kind, part, t).start()
+
+    def weight_wait(kind, part):
+        for t in range(1, 4):
+            x = lax.rem(col_x + t, 4)
+            place = block(kind, part, pl.ds(pl.multiple_of(x * 2 * CH, 2 * CH), 2 * CH))
+            pltpu.make_async_copy(place, place, r_x.at[kind, part, x]).wait()
+
+    def weight_sent(kind):
+        shard_sent(kind)
+        for part in range(2):
+            for t in range(1, 4):
+                block_copy(kind, part, t).wait_send()
+
+    shard_start(0)
     table_start(0, 0)
-    weight_start(0)
-    weight_start(1)
+    shard_start(1)
     table_start(1, 0)
+    for part in range(2):
+        for kind in range(2):
+            block_start(kind, part)
     for k in range(1, 4):
         table_start(0, k)
         table_start(1, k)
@@ -188,6 +224,57 @@
             src_ref=buf.at[rows, col(n)], dst_ref=dst.at[rows, col(n)], send_sem=ss.at[i, n], recv_sem=rs.at[i, n],
             device_id=dev, device_id_type=MESH,
         )
+
+    def rows_refs(kind, part, b, j):
+        at = pl.ds(b * BROWS, BROWS)
+        feat = pl.ds(pl.multiple_of(j * CH, CH), CH)
+        if kind == 0:
+            return xs.at[part, at, feat]
+        if kind == 1:
+            return act.at[part, at, :]
+        if kind == 2:
+            return vee.at[part, at, :]
+        return (um, uin)[part].at[at, feat]
+
+    def rows_copy(kind, b, part, j):
+        dst = (gx, ga, gv, gw)[kind].at[b, pl.ds(pl.multiple_of(chip * BROWS, BROWS), BROWS), :]
+        return rows_refs(kind, part, b, j), dst, s_g.at[kind, b, part, j], r_g.at[kind, b, chip], (2 * z + part, 8 * c + j)
+
+    def rows_each(kind, b, own, far):
+        for part in range(2):
+            def one(t, carry):
+                j = lax.rem(q + t, 8)
+                src, dst, ssem, rsem, dev = rows_copy(kind, b, part, j)
+                mine = jnp.logical_and(h == part, 8 * c + j == e)
+                remote = pltpu.make_async_remote_copy(
+                    src_ref=src, dst_ref=dst, send_sem=ssem, recv_sem=rsem, device_id=dev, device_id_type=MESH
+                )
+                if own:
+                    @pl.when(mine)
+                    def _():
+                        pltpu.make_async_copy(src, dst, rsem).start()
+
+                @pl.when(jnp.logical_not(mine))
+                def _():
+                    far(remote)
+
+                return carry
+
+            lax.fori_loop(0, 8, one, 0)
+
+    def rows_start(kind, b):
+        rows_each(kind, b, True, lambda copy: copy.start())
+
+    def rows_sent(kind, b):
+        rows_each(kind, b, False, lambda copy: copy.wait_send())
+
+    def rows_wait(kind, b):
+        def one(t, carry):
+            place = (gx, ga, gv, gw)[kind].at[b, pl.ds(pl.multiple_of(t * BROWS, BROWS), BROWS), :]
+            pltpu.make_async_copy(place, place, r_g.at[kind, b, t]).wait()
+            return carry
+
+        lax.fori_loop(0, 16, one, 0)
 
     def forward(i, carry):
         rows = pl.ds(pl.multiple_of(i * TOK, TOK), TOK)
@@ -271,6 +358,15 @@
 
     lax.fori_loop(0, MB, forward, 0)
 
+    def early():
+        for b in range(BATCHES):
+            rows_start(0, b)
+            rows_start(1, b)
+
+    @pl.when(z < STAGES - 1)
+    def _():
+        early()
+
     def backward(i, carry):
         rows = pl.ds(pl.multiple_of(i * TOK, TOK), TOK)
         acc = jnp.zeros((TOK, RANK), F32)
@@ -324,77 +420,34 @@
 
         return carry
 
-    lax.fori_loop(0, MB, backward, 0)
-
-    def grad_copies(t):
-        place = lax.rem(chip + t, 16)
-        dev = (2 * z + lax.div(place, 8), 8 * c + lax.rem(place, 8))
-        return [
-            pltpu.make_async_remote_copy(
-                src_ref=src.at[t], dst_ref=dst.at[chip], send_sem=s_g.at[kind, t], recv_sem=r_g.at[kind, chip],
-                device_id=dev, device_id_type=MESH,
-            )
-            for kind, src, dst in ((0, gds, gdl), (1, gus, gul))
-        ]
-
-    def is_me(t):
-        place = lax.rem(chip + t, 16)
-        return jnp.logical_and(lax.div(place, 8) == h, 8 * c + lax.rem(place, 8) == e)
-
-    def grads(t, carry):
-        place = lax.rem(chip + t, 16)
-        part, at = lax.div(place, 8), pl.ds(pl.multiple_of(lax.rem(place, 8) * CH, CH), CH)
-        gds[t] = tn(xs[part, :, at], vee[part, :, :]).astype(BF16)
-
-        @pl.when(part == 0)
-        def _():
-            gus[t] = tn(act[0], um[:, at]).astype(BF16)
-
-        @pl.when(part == 1)
-        def _():
-            gus[t] = tn(act[1], uin[:, at]).astype(BF16)
-
-        @pl.when(is_me(t))
-        def _():
-            gdl[chip] = gds[t]
-            gul[chip] = gus[t]
-
-        @pl.when(jnp.logical_not(is_me(t)))
-        def _():
-            for copy in grad_copies(t):
-                copy.start()
-
-        return carry
-
-    lax.fori_loop(0, 16, grads, 0)
+    for b in range(BATCHES):
+        lax.fori_loop(b * MB // BATCHES, (b + 1) * MB // BATCHES, backward, 0)
+        rows_start(2, b)
+        rows_start(3, b)
+
+    @pl.when(z == STAGES - 1)
+    def _():
+        early()
+
+    def total(b):
+        def one(n, carry):
+            at = pl.ds(pl.multiple_of(n * 256, 256), 256)
+            gd_out[...] += tn(gx[b, at, :], gv[b, at, :])
+            gu_out[...] += tn(ga[b, at, :], gw[b, at, :])
+            return carry
+
+        lax.fori_loop(0, 16 * BROWS // 256, one, 0)
 
     gd_out[...] = jnp.zeros_like(gd_out)
     gu_out[...] = jnp.zeros_like(gu_out)
-
-    def gather(t, carry):
-        place = lax.rem(chip + 16 - t, 16)
-
-        @pl.when(jnp.logical_not(jnp.logical_and(local, t == 0)))
-        def _():
-            for kind, dst in ((0, gdl), (1, gul)):
-                ref = dst.at[place]
-                pltpu.make_async_copy(ref, ref, r_g.at[kind, place]).wait()
-
-        gd_out[...] += gdl[place].astype(F32)
-        gu_out[...] += gul[place].astype(F32)
-        return carry
-
-    lax.fori_loop(0, 16, gather, 0)
-
-    def grads_sent(t, carry):
-        @pl.when(jnp.logical_not(is_me(t)))
-        def _():
-            for copy in grad_copies(t):
-                copy.wait_send()
-
-        return carry
-
-    lax.fori_loop(0, 16, grads_sent, 0)
+    for b in range(BATCHES):
+        for kind in range(4):
+            rows_wait(kind, b)
+        total(b)
+
+    for b in range(BATCHES):
+        for kind in range(4):
+            rows_sent(kind, b)
     weight_sent(0)
     weight_sent(1)
     for k in range(4):
@@ -419,14 +472,12 @@
 
 
 def shards(tokens, cotangent, sample_ids, sent_before, received_before, norm_gain, down_proj, up_proj):
-    s = lax.axis_index("section")
     e = lax.axis_index("dp")
-    last = lax.axis_size("section") - 1
     ids = sample_ids[0]
     micro = jnp.arange(MB, dtype=jnp.int32)
     where_is = jnp.sum(jnp.where(ids[None, :] == micro[:, None], micro[None, :], 0), axis=1)
-    rec = jnp.where(s == 0, jnp.take(tokens, where_is, axis=0, mode="clip"), received_before[0])
-    sent = jnp.where(s == last, jnp.take(cotangent, where_is, axis=0, mode="clip"), sent_before[0])
+    tok = jnp.take(tokens, where_is, axis=0, mode="clip")
+    cot = jnp.take(cotangent, where_is, axis=0, mode="clip")
     gain = lax.dynamic_slice(norm_gain[0], (e * CH,), (CH,))[:, None]
     down = (down_proj[0].astype(F32) * gain).astype(BF16)
     any_ = pl.BlockSpec(memory_space=pl.ANY)
@@ -436,7 +487,7 @@
     grad_down, grad_up = pl.pallas_call(
         kernel,
         out_shape=(jax.ShapeDtypeStruct((CH, RANK), F32), jax.ShapeDtypeStruct((RANK, CH), F32)),
-        in_specs=[any_] * 4,
+        in_specs=[any_] * 6,
         out_specs=(vmem, vmem),
         scratch_shapes=[
             pltpu.VMEM((2, rows, HALF), BF16),
@@ -456,21 +507,22 @@
             pltpu.VMEM((2, rows, RANK), BF16),
             pltpu.VMEM((2, rows, RANK), BF16),
             pltpu.VMEM((2, rows, 128), F32),
-            pltpu.VMEM((16, CH, RANK), BF16),
-            pltpu.VMEM((16, RANK, CH), BF16),
-            pltpu.VMEM((16, CH, RANK), BF16),
-            pltpu.VMEM((16, RANK, CH), BF16),
+            pltpu.VMEM((BATCHES, 16 * BROWS, CH), BF16),
+            pltpu.VMEM((BATCHES, 16 * BROWS, RANK), BF16),
+            pltpu.VMEM((BATCHES, 16 * BROWS, RANK), BF16),
+            pltpu.VMEM((BATCHES, 16 * BROWS, CH), BF16),
             dma((2, 4, 4)), dma((2, 2, MB)),
-            dma((2, 16)), dma((2, 2, 8)),
+            dma((2, 4)), dma((2, 2, 2)),
+            dma((2, 2, 4)), dma((2, 2, 4)),
             dma((MB, NCOL)), dma((MB, NCOL)),
             dma((MB, NCOL)), dma((MB, NCOL)),
             dma((4 * MB,)), dma((4 * MB,)),
-            dma((2, 16)), dma((2, 16)),
+            dma((4, BATCHES, 2, 8)), dma((4, BATCHES, 16)),
         ],
         compiler_params=pltpu.CompilerParams(
             collective_id=0, has_side_effects=True, vmem_limit_bytes=56 * 1024 * 1024
         ),
-    )(rec, sent, down, up_proj[0])
+    )(received_before[0], sent_before[0], tok, cot, down, up_proj[0])
     return ((grad_down * gain)[None], grad_up[None])
 
 

time: 485 us -> 343 us (0.71)
  Pallas kernels: 463 us -> 329 us
  other arithmetic: 9.92 us -> 4.68 us
    pallas_call x1, Pallas kernels: 463 us -> 329 us  [shards(): pl.pallas_call(kernel, out_shape=(jax.ShapeDtypeStruct((CH, RANK), F32),...]
    select_n x1 -> x0, other arithmetic: 5.24 us -> none  [shards(): jnp.where(s == last, jnp.take(cotangent, where_is, axis=0, mode='clip'),...]
where the time goes in v2:
time: 343 us; the launch traced here: 342 us
  Pallas kernels  329 us (96%)
  local copies, waits for them, and re-layouts  8.15 us (2%)
  other arithmetic  4.68 us (1%)
    pallas_call x1, Pallas kernels, shards(): pl.pallas_call(kernel, out_shape=(jax.ShapeDtypeStruct((CH, RANK), F32),...  329 us

profile of v2, /device:TPU:1, one launch (start us, length us, event | category | flops | bytes accessed | tf_op | source)
XLA Modules:
  0.0 342.2 jit_solution(5080319426045922059)
XLA Ops:
  0.6 0.0 copy-start
  0.6 0.9 select_reduce_fusion
  1.6 0.7 constant_dynamic-slice_fusion
  2.3 1.8 fusion.down_in
  4.0 0.0 copy-done
  4.0 2.0 gather_fusion.1
  6.0 3.6 %gather_fusion = bf16[8,16,8192]{2,1,0:T(8,128)(2,1)} fusion(bf16[8,16,8192]{2,1,0:T(8,128)(2,1)} %param.8, s32[1024]{0:T(1024)S(1)} %pad_clamp_fusion), kind=kCustom, calls=%fused_computation | custom fusion | bytes 4194336 | tf_op jit(solution)/shard_map/jit(_take)/gather | solution.py:479
  9.6 328.8 %shard_map.95 = (f32[512,256]{1,0:T(8,128)}, f32[256,512]{1,0:T(8,128)}) custom-call(bf16[8,16,8192]{2,1,0:T(8,128)(2,1)} %bitcast.11, bf16[8,16,8192]{2,1,0:T(8,128)(2,1)} %bitcast.12, bf16[8,16,8192]{2,1,0:T(8,128)(2,1)} %gather_fusion, bf16[8,16,8192]{2,1,0:T(8,128)(2,1)} %gather_fusion.1, bf16[512,256]{1,0:T(8,128)(2,1)} %fusion.down_in, ...), custom_call_target="tpu_custom_call" | custom-call | tf_op jit(solution)/shard_map/pallas_call | solution.py:487
  338.4 2.0 multiply_bitcast_fusion
  340.4 1.9 copy.11
  (1 shorter events, 0.0 us)
Async XLA Ops:
  0.6 3.4 copy-start

commit v3 on v1

v3 whole, which is shorter than its diff:
```python
import functools

import jax
import jax.numpy as jnp
from jax import lax
from jax.experimental import pallas as pl
from jax.experimental.pallas import tpu as pltpu
from jax.sharding import PartitionSpec as P

MESH = pl.DeviceIdType.MESH
F32, BF16 = jnp.float32, jnp.bfloat16
EPS = 1e-05
D = 8192
HALF = 4096
RANK = 256
TOK = 16
MB = 8
CH = 512
COLS = 512
NCOL = HALF // COLS
STAGES = 8
BATCH = 2 * TOK
NBATCH = MB * TOK // BATCH
PACK = CH + RANK


def tn(a, b):
    return lax.dot_general(a, b, (((0,), (0,)), ((), ())), preferred_element_type=F32)


def nn(a, b):
    return jnp.dot(a, b, preferred_element_type=F32)


def lanes(v):
    total = v[:, 0:128]
    for k in range(128, v.shape[1], 128):
        total = total + v[:, k : k + 128]
    return total


def kernel(
    ids, rec_in, sent_in, tok_in, cot_in, gain_in, down_in, up_in, gd_out, gu_out,
    raw, perm, gn, rec, sent, wd, wu, wdt, wut, xin, xz, uz, xf, fout, bout, red_tx, red_rx,
    pre, scl, gxz, guz,
    c_raw, s_tok, s_gn, r_gn, s_tab, r_tab, s_w, r_w, s_x, r_x, s_xr, r_xr,
    s_u, r_u, s_v, r_v, s_vr, r_vr,
    s_hf, r_hf, s_hb, r_hb, s_red, r_red, s_g, r_g,
):
    s = lax.axis_index("section")
    e = lax.axis_index("dp")
    h, z = lax.rem(s, 2), lax.div(s, 2)
    c, q = lax.rem(e, 2), lax.div(e, 2)
    chip = h * 8 + q
    owner_core = lax.div(e, 8)
    local = c == owner_core
    other = (s, e + 1 - 2 * c)

    raw_tok = pltpu.make_async_copy(tok_in, raw, c_raw)
    raw_cot = pltpu.make_async_copy(cot_in, raw, c_raw)

    @pl.when(z == 0)
    def _():
        raw_tok.start()

    @pl.when(z == STAGES - 1)
    def _():
        raw_cot.start()

    barrier = pltpu.get_barrier_semaphore()

    def greet(t, carry):
        place = lax.rem(h * 16 + e + t, 32)
        pl.semaphore_signal(
            barrier, inc=1, device_id=(2 * z + lax.div(place, 16), lax.rem(place, 16)), device_id_type=MESH
        )
        return carry

    lax.fori_loop(1, 32, greet, 0)

    @pl.when(z > 0)
    def _():
        pl.semaphore_signal(barrier, inc=1, device_id=(s - 2, e), device_id_type=MESH)

    @pl.when(z < STAGES - 1)
    def _():
        pl.semaphore_signal(barrier, inc=1, device_id=(s + 2, e), device_id_type=MESH)

    neighbours = jnp.where(z > 0, 1, 0) + jnp.where(z < STAGES - 1, 1, 0)
    pl.semaphore_wait(barrier, 31 + neighbours)

    def table_copy(which, k, t):
        src = (rec_in, sent_in)[which]
        dst = (rec, sent)[which]
        h2, c2 = lax.rem(h + t // 2, 2), lax.rem(c + t, 2)
        row = pl.multiple_of((2 * k + c) * TOK, TOK)
        return dict(
            src_ref=src.at[4 * h2 + k, :, pl.ds(pl.multiple_of(c2 * HALF, HALF), HALF)],
            dst_ref=dst.at[h, pl.ds(row, TOK), :],
        ), s_tab.at[which, k, t], r_tab.at[which, h, 2 * k + c], (2 * z + h2, 2 * q + c2)

    def table_used(which):
        return s != (0, 2 * STAGES - 1)[which]

    def table_start(which, k):
        @pl.when(table_used(which))
        def _():
            for t in range(4):
                refs, ssem, rsem, dev = table_copy(which, k, t)
                if t == 0:
                    pltpu.make_async_copy(refs["src_ref"], refs["dst_ref"], rsem).start()
                else:
                    pltpu.make_async_remote_copy(
                        **refs, send_sem=ssem, recv_sem=rsem, device_id=dev, device_id_type=MESH
                    ).start()

    def table_sent(which, k):
        @pl.when(table_used(which))
        def _():
            for t in range(1, 4):
                refs, ssem, rsem, dev = table_copy(which, k, t)
                pltpu.make_async_remote_copy(
                    **refs, send_sem=ssem, recv_sem=rsem, device_id=dev, device_id_type=MESH
                ).wait_send()

    def end_copies(which, k):
        dst, part = ((rec, 0), (sent, 1))[which]
        place = dst.at[part, pl.ds(pl.multiple_of((2 * k + c) * TOK, TOK), TOK), :]
        rsem = r_tab.at[which, part, 2 * k + c]
        mine = perm.at[k, :, pl.ds(pl.multiple_of(c * HALF, HALF), HALF)]
        return mine, place, rsem

    def end_far(which, k):
        theirs = perm.at[k, :, pl.ds(pl.multiple_of((1 - c) * HALF, HALF), HALF)]
        place, rsem = end_copies(which, k)[1:]
        return pltpu.make_async_remote_copy(
            src_ref=theirs, dst_ref=place, send_sem=s_tok.at[k], recv_sem=rsem, device_id=other, device_id_type=MESH
        )

    def end_start(which):
        (raw_tok, raw_cot)[which].wait()
        for k in range(4):
            at = jnp.int32(0)
            for m in range(1, MB):
                at = jnp.where(ids[0, m] == 4 * h + k, m, at)
            at = jnp.clip(at, 0, MB - 1)

            def move(n, carry, at=at, k=k):
                cols = pl.ds(pl.multiple_of(n * 1024, 1024), 1024)
                perm[k, :, cols] = raw[at, :, cols]
                return carry

            lax.fori_loop(0, D // 1024, move, 0)
            end_far(which, k).start()
            pltpu.make_async_copy(*end_copies(which, k)).start()

    def end_sent(which):
        for k in range(4):
            end_far(which, k).wait_send()

    def table_wait(which, part, i):
        place = (rec, sent)[which].at[part, pl.ds(pl.multiple_of(i * TOK, TOK), TOK), :]
        pltpu.make_async_copy(place, place, r_tab.at[which, part, i]).wait()

    slot = lax.rem(e, 8)
    spot = pl.ds(pl.multiple_of(slot * CH, CH), CH)
    col_x = lax.rem(q, 4)
    row_y = 2 * h + owner_core

    def device(x, y, core):
        return (2 * z + lax.div(y, 2), 8 * lax.rem(y, 2) + 2 * x + core)

    def wide(x):
        return pl.ds(pl.multiple_of(x * 2 * CH, 2 * CH), 2 * CH)

    def away(t):
        return lax.rem(col_x + t, 4)

    def w_remote(t):
        return pltpu.make_async_remote_copy(
            src_ref=down_in, dst_ref=wd.at[h, spot, :], send_sem=s_w.at[t], recv_sem=r_w.at[h, c],
            device_id=device(col_x, lax.rem(row_y + t, 4), owner_core), device_id_type=MESH,
        )

    def u_remote(t):
        return pltpu.make_async_remote_copy(
            src_ref=up_in, dst_ref=wu.at[h, :, spot], send_sem=s_u.at[t], recv_sem=r_u.at[slot],
            device_id=device(away(t), row_y, owner_core), device_id_type=MESH,
        )

    def first_start():
        @pl.when(local)
        def _():
            pltpu.make_async_copy(down_in, wd.at[h, spot, :], r_w.at[h, c]).start()

        @pl.when(jnp.logical_not(local))
        def _():
            w_remote(0).start()

        for t in (1, 3, 2):
            w_remote(t).start()

        @pl.when(local)
        def _():
            pltpu.make_async_copy(up_in, wu.at[h, :, spot], r_u.at[slot]).start()

        @pl.when(jnp.logical_not(local))
        def _():
            u_remote(0).start()

        for t in (1, 3, 2):
            u_remote(t).start()

    def first_sent():
        @pl.when(jnp.logical_not(local))
        def _():
            w_remote(0).wait_send()
            u_remote(0).wait_send()

        for t in range(1, 4):
            w_remote(t).wait_send()
            u_remote(t).wait_send()

    def w_block(part, t):
        place = wd.at[part, wide(col_x), :]
        return pltpu.make_async_remote_copy(
            src_ref=place, dst_ref=place, send_sem=s_x.at[part, t], recv_sem=r_x.at[part, col_x],
            device_id=(s, e - 2 * col_x + 2 * away(t)), device_id_type=MESH,
        )

    def w_start(part):
        for j in range(2):
            place = wd.at[part, pl.ds(pl.multiple_of((2 * col_x + j) * CH, CH), CH), :]
            pltpu.make_async_copy(place, place, r_w.at[part, j]).wait()
        for t in (1, 3):
            w_block(part, t).start()

    def w_half(part, x, half):
        return wd.at[part, pl.ds(pl.multiple_of((2 * x + half) * CH, CH), CH), :]

    def w_relay(part, half):
        place = w_half(part, away((3, 1)[half]), half)
        return pltpu.make_async_remote_copy(
            src_ref=place, dst_ref=place, send_sem=s_xr.at[part, half], recv_sem=r_xr.at[part, half],
            device_id=(s, e - 2 * col_x + 2 * away((1, 3)[half])), device_id_type=MESH,
        )

    def w_forward(part):
        for half in range(2):
            x = away((3, 1)[half])
            place = wd.at[part, wide(x), :]
            pltpu.make_async_copy(place, place, r_x.at[part, x]).wait()
            w_relay(part, half).start()

    def u_block(n, t):
        place = wu.at[h, :, wide(away(n))]
        return pltpu.make_async_remote_copy(
            src_ref=place, dst_ref=place, send_sem=s_v.at[n, t], recv_sem=r_v.at[h, away(n)],
            device_id=device(col_x, lax.rem(row_y + t, 4), c), device_id_type=MESH,
        )

    def u_start(n):
        @pl.when(local)
        def _():
            for j in range(2):
                at = 2 * away(n) + j
                place = wu.at[h, :, pl.ds(pl.multiple_of(at * CH, CH), CH)]
                pltpu.make_async_copy(place, place, r_u.at[at]).wait()
            for t in (1, 3):
                u_block(n, t).start()

    y_me = 2 * h + lax.div(e, 8)

    def u_half(part, n, half):
        return wu.at[part, pl.ds(pl.multiple_of(half * (RANK // 2), RANK // 2), RANK // 2), wide(away(n))]

    def u_relay(part, n):
        half = jnp.where(lax.rem(y_me - 2 * part - c + 4, 4) == 1, 0, 1)
        place = u_half(part, n, half)
        return pltpu.make_async_remote_copy(
            src_ref=place, dst_ref=place, send_sem=s_vr.at[part, n], recv_sem=r_vr.at[n, half],
            device_id=device(col_x, lax.rem(y_me + 1 + 2 * half, 4), c), device_id_type=MESH,
        )

    def u_forward(n):
        @pl.when(jnp.logical_not(local))
        def _():
            for part in range(2):
                place = wu.at[part, :, wide(away(n))]
                pltpu.make_async_copy(place, place, r_v.at[part, away(n)]).wait()
                u_relay(part, n).start()

    def weight_wait(kind, part):
        if kind == 0:
            for half in range(2):
                place = w_half(part, away(2), half)
                pltpu.make_async_copy(place, place, r_xr.at[part, half]).wait()
        else:
            @pl.when(jnp.logical_and(local, h != part))
            def _():
                for n in range(4):
                    for half in range(2):
                        place = u_half(part, n, half)
                        pltpu.make_async_copy(place, place, r_vr.at[n, half]).wait()

    def weight_sent():
        first_sent()
        for part in range(2):
            for t in (1, 3):
                w_block(part, t).wait_send()
            for half in range(2):
                w_relay(part, half).wait_send()

        @pl.when(local)
        def _():
            for n in range(4):
                for t in (1, 3):
                    u_block(n, t).wait_send()

        @pl.when(jnp.logical_not(local))
        def _():
            for n in range(4):
                for part in range(2):
                    u_relay(part, n).wait_send()

    gain_part = gain_in.at[:, pl.ds(pl.multiple_of(c * HALF, HALF), HALF)]
    gain_near = pltpu.make_async_copy(gain_part, gn.at[h], r_gn.at[h])
    gain_far = pltpu.make_async_remote_copy(
        src_ref=gain_part, dst_ref=gn.at[h], send_sem=s_gn, recv_sem=r_gn.at[h],
        device_id=(s + 1 - 2 * h, e), device_id_type=MESH,
    )

    first_start()
    gain_near.start()
    gain_far.start()
    table_start(0, 0)
    table_start(1, 0)

    @pl.when(z == 0)
    def _():
        end_start(0)

    @pl.when(z == STAGES - 1)
    def _():
        end_start(1)

    w_start(0)
    u_start(0)
    w_start(1)
    for n in (1, 3, 2):
        u_start(n)
    w_forward(0)
    u_forward(0)
    w_forward(1)
    u_forward(1)
    u_forward(3)
    table_start(0, 1)
    table_start(1, 1)
    u_forward(2)
    for k in range(2, 4):
        table_start(0, k)
        table_start(1, k)
    for part in range(2):
        pltpu.make_async_copy(gn.at[part], gn.at[part], r_gn.at[part]).wait()

    def red_copy(n):
        return pltpu.make_async_remote_copy(
            src_ref=red_tx.at[n], dst_ref=red_rx.at[n], send_sem=s_red.at[n], recv_sem=r_red.at[n],
            device_id=other, device_id_type=MESH,
        )

    def col(n):
        return slice(n * COLS, (n + 1) * COLS)

    def hop(n, i, ahead):
        rows = pl.ds(pl.multiple_of(i * TOK, TOK), TOK)
        if ahead:
            wide_col = slice(2 * n * COLS, 2 * (n + 1) * COLS)
            src, dst, ss, rs, dev = fout.at[rows, wide_col], xin.at[rows, wide_col], s_hf, r_hf, (s + 2, e)
        else:
            two = pl.ds(2 * n, 2)
            src, dst, ss, rs, dev = bout.at[two, rows, :], uz.at[1, two, rows, pl.ds(0, CH)], s_hb, r_hb, (s - 2, e)
        return pltpu.make_async_remote_copy(
            src_ref=src, dst_ref=dst, send_sem=ss.at[i, n], recv_sem=rs.at[i, n], device_id=dev, device_id_type=MESH
        )

    def rows_copy(kind, b, part, j):
        src = (xz, uz)[kind].at[part, j, pl.ds(pl.multiple_of(b * BATCH, BATCH), BATCH), :]
        return src, landing(kind, b, chip), s_g.at[kind, b, part, j], r_g.at[kind, b, chip], (2 * z + part, 8 * c + j)

    def landing(kind, b, source):
        at = pl.ds(pl.multiple_of((16 * b + source) * BATCH, BATCH), BATCH)
        return (gxz, guz)[kind].at[at, :]

    def rows_each(kind, b, own, far):
        def one(t, carry):
            place = lax.rem(chip + t, 16)
            part, j = lax.div(place, 8), lax.rem(place, 8)
            src, dst, ssem, rsem, dev = rows_copy(kind, b, part, j)
            mine = jnp.logical_and(h == part, 8 * c + j == e)
            if own:
                @pl.when(mine)
                def _():
                    pltpu.make_async_copy(src, dst, rsem).start()

            @pl.when(jnp.logical_not(mine))
            def _():
                far(
                    pltpu.make_async_remote_copy(
                        src_ref=src, dst_ref=dst, send_sem=ssem, recv_sem=rsem, device_id=dev, device_id_type=MESH
                    )
                )

            return carry

        lax.fori_loop(0, 16, one, 0)

    def rows_start(kind, b):
        rows_each(kind, b, True, lambda copy: copy.start())

    def rows_sent(kind, b):
        rows_each(kind, b, False, lambda copy: copy.wait_send())

    def rows_wait(kind, b):
        def one(t, carry):
            place = landing(kind, b, t)
            pltpu.make_async_copy(place, place, r_g.at[kind, b, t]).wait()
            return carry

        lax.fori_loop(0, 16, one, 0)

    def turn():
        for part in range(2):
            def one(j, carry, part=part):
                at = pl.ds(pl.multiple_of(j * CH, CH), CH)
                wdt[part, :, at] = wd[part, at, :].T
                wut[part, at, :] = wu[part, :, at].T
                return carry

            lax.fori_loop(0, HALF // CH, one, 0)

    late = z >= STAGES // 2

    @pl.when(late)
    def _():
        for kind in range(2):
            for part in range(2):
                weight_wait(kind, part)
        turn()

    def forward(i, carry):
        rows = pl.ds(pl.multiple_of(i * TOK, TOK), TOK)
        fresh = jnp.logical_and(i == 0, jnp.logical_not(late))
        table_wait(0, 0, i)

        @pl.when(fresh)
        def _():
            weight_wait(0, 0)

        acc = jnp.zeros((TOK, RANK), F32)
        sq = jnp.zeros((TOK, 128), F32)
        for n in range(NCOL):
            @pl.when(z > 0)
            def _():
                if n % 2 == 0:
                    hop(n // 2, i, True).wait_recv()
                xf[:, col(n)] = rec[0, rows, col(n)].astype(F32) + xin[rows, col(n)].astype(F32)

            @pl.when(z == 0)
            def _():
                xf[:, col(n)] = rec[0, rows, col(n)].astype(F32)

            x = xf[:, col(n)]
            xz[0, n, rows, 0:CH] = x.astype(BF16)
            sq = sq + lanes(x * x)
            acc = acc + nn((x * gn[0, :, col(n)]).astype(BF16), wd[0, col(n), :])

        def finish(part, acc, sq):
            n = 2 * i + part
            red_tx[n, :, 0:RANK] = acc
            red_tx[n, :, RANK:] = sq
            red_copy(n).start()
            red_copy(n).wait_recv()
            total = acc + red_rx[n, :, 0:RANK]
            square = jnp.sum(sq + red_rx[n, :, RANK:], axis=1, keepdims=True)
            scale = lax.rsqrt(square * (1.0 / D) + EPS)
            v = total * scale
            pre[part, rows, :] = v
            scl[part, rows, :] = jnp.broadcast_to(scale, (TOK, 128))
            a = (v * jax.nn.sigmoid(v)).astype(BF16)
            for j in range(8):
                xz[part, j, rows, CH:] = a
            return a

        a = finish(0, acc, sq)

        @pl.when(fresh)
        def _():
            weight_wait(1, 0)
            weight_wait(0, 1)

        table_wait(0, 1, i)
        table_wait(1, 0, i)
        acc = jnp.zeros((TOK, RANK), F32)
        sq = jnp.zeros((TOK, 128), F32)
        for n in range(NCOL):
            x = (
                xf[:, col(n)] + nn(a, wu[0, :, col(n)])
                + (rec[1, rows, col(n)].astype(F32) - sent[0, rows, col(n)].astype(F32))
            )
            xf[:, col(n)] = x
            xz[1, n, rows, 0:CH] = x.astype(BF16)
            sq = sq + lanes(x * x)
            acc = acc + nn((x * gn[1, :, col(n)]).astype(BF16), wd[1, col(n), :])
        a = finish(1, acc, sq)

        @pl.when(fresh)
        def _():
            weight_wait(1, 1)

        table_wait(1, 1, i)

        @pl.when(z < STAGES - 1)
        def _():
            for n in range(NCOL):
                x = xf[:, col(n)] + nn(a, wu[1, :, col(n)]) - sent[1, rows, col(n)].astype(F32)
                fout[rows, col(n)] = x.astype(BF16)
                if n % 2 == 1:
                    hop(n // 2, i, True).start()

        return carry

    lax.fori_loop(0, MB, forward, 0)

    @pl.when(jnp.logical_not(late))
    def _():
        turn()

    def early():
        def one(b, carry):
            rows_start(0, b)
            return carry

        lax.fori_loop(0, NBATCH, one, 0)

    @pl.when(z < STAGES - 1)
    def _():
        early()

    def backward(i, carry):
        rows = pl.ds(pl.multiple_of(i * TOK, TOK), TOK)
        acc = jnp.zeros((TOK, RANK), F32)
        for n in range(NCOL):
            if n % 2 == 0:
                @pl.when(z < STAGES - 1)
                def _():
                    hop(n // 2, i, False).wait_recv()

            @pl.when(z == STAGES - 1)
            def _():
                uz[1, n, rows, 0:CH] = sent[1, rows, col(n)]

            acc = acc + nn(uz[1, n, rows, 0:CH], wut[1, col(n), :])

        def finish(part, acc):
            n = 2 * MB + 2 * i + part
            red_tx[n, :, 0:RANK] = acc
            red_tx[n, :, RANK:] = jnp.zeros((TOK, 128), F32)
            red_copy(n).start()
            red_copy(n).wait_recv()
            total = acc + red_rx[n, :, 0:RANK]
            v = pre[part, rows, :]
            gate = jax.nn.sigmoid(v)
            d_pre = total * gate * (1.0 + v * (1.0 - gate))
            scale = scl[part, rows, 0:1]
            mean = jnp.sum(d_pre * v, axis=1, keepdims=True) * (1.0 / D)
            back = (d_pre * scale).astype(BF16)
            for j in range(8):
                uz[part, j, rows, CH:] = back
            return back, mean * scale * scale

        back, shrink = finish(1, acc)
        acc = jnp.zeros((TOK, RANK), F32)
        for n in range(NCOL):
            u = (
                uz[1, n, rows, 0:CH].astype(F32) + nn(back, wdt[1, :, col(n)]) * gn[1, :, col(n)]
                - shrink * xz[1, n, rows, 0:CH].astype(F32)
            ).astype(BF16)
            uz[0, n, rows, 0:CH] = u
            acc = acc + nn(u, wut[0, col(n), :])
        back, shrink = finish(0, acc)

        @pl.when(z > 0)
        def _():
            for n in range(NCOL):
                u = (
                    uz[0, n, rows, 0:CH].astype(F32) + nn(back, wdt[0, :, col(n)]) * gn[0, :, col(n)]
                    - shrink * xz[0, n, rows, 0:CH].astype(F32)
                )
                bout[n, rows, :] = u.astype(BF16)
                if n % 2 == 1:
                    hop(n // 2, i, False).start()

        return carry

    def back_batch(b, carry):
        lax.fori_loop(b * (BATCH // TOK), (b + 1) * (BATCH // TOK), backward, 0)
        rows_start(1, b)
        return carry

    lax.fori_loop(0, NBATCH, back_batch, 0)

    @pl.when(z == STAGES - 1)
    def _():
        early()

    gd_out[...] = jnp.zeros_like(gd_out)
    gu_out[...] = jnp.zeros_like(gu_out)

    def total(b, carry):
        rows_wait(0, b)
        rows_wait(1, b)
        at = pl.ds(pl.multiple_of(16 * BATCH * b, 16 * BATCH), 16 * BATCH)
        gd_out[...] += tn(gxz[at, 0:CH], guz[at, CH:])
        gu_out[...] += tn(gxz[at, CH:], guz[at, 0:CH])
        return carry

    lax.fori_loop(0, NBATCH, total, 0)

    def all_rows_sent(b, carry):
        rows_sent(0, b)
        rows_sent(1, b)
        return carry

    lax.fori_loop(0, NBATCH, all_rows_sent, 0)
    weight_sent()
    gain_far.wait_send()

    @pl.when(z == 0)
    def _():
        end_sent(0)

    @pl.when(z == STAGES - 1)
    def _():
        end_sent(1)

    for k in range(4):
        table_sent(0, k)
        table_sent(1, k)

    def rest(i, carry):
        for n in range(NCOL // 2):
            @pl.when(z < STAGES - 1)
            def _():
                hop(n, i, True).wait_send()

            @pl.when(z > 0)
            def _():
                hop(n, i, False).wait_send()

        for k in range(4):
            red_copy(4 * i + k).wait_send()
        return carry

    lax.fori_loop(0, MB, rest, 0)


def shards(tokens, cotangent, sample_ids, sent_before, received_before, norm_gain, down_proj, up_proj):
    e = lax.axis_index("dp")
    gain = lax.dynamic_slice(norm_gain[0], (e * CH,), (CH,))[:, None]
    any_ = pl.BlockSpec(memory_space=pl.ANY)
    vmem = pl.BlockSpec(memory_space=pltpu.VMEM)
    dma = pltpu.SemaphoreType.DMA
    rows = MB * TOK
    grad_down, grad_up = pl.pallas_call(
        kernel,
        out_shape=(jax.ShapeDtypeStruct((CH, RANK), F32), jax.ShapeDtypeStruct((RANK, CH), F32)),
        in_specs=[pl.BlockSpec(memory_space=pltpu.SMEM)] + [any_] * 7,
        out_specs=(vmem, vmem),
        scratch_shapes=[
            pltpu.VMEM((MB, TOK, D), BF16),
            pltpu.VMEM((4, TOK, D), BF16),
            pltpu.VMEM((2, 1, HALF), F32),
            pltpu.VMEM((2, rows, HALF), BF16),
            pltpu.VMEM((2, rows, HALF), BF16),
            pltpu.VMEM((2, HALF, RANK), BF16),
            pltpu.VMEM((2, RANK, HALF), BF16),
            pltpu.VMEM((2, RANK, HALF), BF16),
            pltpu.VMEM((2, HALF, RANK), BF16),
            pltpu.VMEM((rows, HALF), BF16),
            pltpu.VMEM((2, 8, rows, PACK), BF16),
            pltpu.VMEM((2, 8, rows, PACK), BF16),
            pltpu.VMEM((TOK, HALF), F32),
            pltpu.VMEM((rows, HALF), BF16),
            pltpu.VMEM((8, rows, CH), BF16),
            pltpu.VMEM((4 * MB, TOK, RANK + 128), F32),
            pltpu.VMEM((4 * MB, TOK, RANK + 128), F32),
            pltpu.VMEM((2, rows, RANK), F32),
            pltpu.VMEM((2, rows, 128), F32),
            pltpu.VMEM((16 * rows, PACK), BF16),
            pltpu.VMEM((16 * rows, PACK), BF16),
            dma, dma((4,)),
            dma, dma((2,)),
            dma((2, 4, 4)), dma((2, 2, MB)),
            dma((4,)), dma((2, 2)), dma((2, 4)), dma((2, 4)), dma((2, 2)), dma((2, 2)),
            dma((4,)), dma((8,)), dma((4, 4)), dma((2, 4)), dma((2, 4)), dma((4, 2)),
            dma((MB, NCOL // 2)), dma((MB, NCOL // 2)),
            dma((MB, NCOL // 2)), dma((MB, NCOL // 2)),
            dma((4 * MB,)), dma((4 * MB,)),
            dma((2, NBATCH, 2, 8)), dma((2, NBATCH, 16)),
        ],
        compiler_params=pltpu.CompilerParams(
            collective_id=0, has_side_effects=True, vmem_limit_bytes=56 * 1024 * 1024
        ),
    )(sample_ids, received_before[0], sent_before[0], tokens, cotangent, norm_gain, down_proj[0], up_proj[0])
    return ((grad_down * gain)[None], grad_up[None])


def solution(mesh):
    placed = (
        P(None, "dp", None),
        P(None, "dp", None),
        P("dp", None),
        P("section", "dp", None, None),
        P("section", "dp", None, None),
        P("section", None),
        P("section", "dp", None),
        P("section", None, "dp"),
    )
    return jax.shard_map(
        shards,
        mesh=mesh,
        in_specs=placed,
        out_specs=(P("section", "dp", None), P("section", None, "dp")),
        check_vma=False,
    )
```

time: 485 us -> 302 us (0.62)
  Pallas kernels: 463 us -> 294 us
  other arithmetic: 9.92 us -> 1.97 us
  local copies, waits for them, and re-layouts: 8.16 us -> 2.55 us
    pallas_call x1, Pallas kernels: 463 us -> 294 us  [shards(): pl.pallas_call(kernel, out_shape=(jax.ShapeDtypeStruct((CH, RANK), F32),...]
    gather x2 -> x0, local copies, waits for them, and re-layouts: 5.6 us -> none  [the longest x1 3.62 us: shards(): jnp.take(tokens, where_is, axis=0, mode='clip')]
    select_n x1 -> x0, other arithmetic: 5.24 us -> none  [shards(): jnp.where(s == last, jnp.take(cotangent, where_is, axis=0, mode='clip'),...]
where the time goes in v3:
time: 302 us; the launch traced here: 299 us
  Pallas kernels  294 us (97%)
    pallas_call x1, Pallas kernels, shards(): pl.pallas_call(kernel, out_shape=(jax.ShapeDtypeStruct((CH, RANK), F32),...  294 us

profile of v3, /device:TPU:1, one launch (start us, length us, event | category | flops | bytes accessed | tf_op | source)
XLA Modules:
  0.0 299.3 jit_solution(7652767425850047830)
XLA Ops:
  0.6 0.7 constant_dynamic-slice_fusion
  1.3 294.2 %shard_map.95 = (f32[512,256]{1,0:T(8,128)}, f32[256,512]{1,0:T(8,128)}) custom-call(s32[1,8]{1,0:T(1,128)} %ids.1, bf16[8,16,8192]{2,1,0:T(8,128)(2,1)} %bitcast.8, bf16[8,16,8192]{2,1,0:T(8,128)(2,1)} %bitcast.9, bf16[8,16,8192]{2,1,0:T(8,128)(2,1)} %tok_in.1, bf16[8,16,8192]{2,1,0:T(8,128)(2,1)} %cot_in.1, f32[1,8192]{1,0:T(1,128)} %gain_in.1, ...), custom_call_target="tpu_custom_call" | custom-call | tf_op jit(solution)/shard_map/pallas_call | solution.py:675
  295.5 2.0 multiply_bitcast_fusion
  297.5 1.9 copy.11

commit v4 on v3

--- a/solution.py
+++ b/solution.py
@@ -42,10 +42,10 @@
 def kernel(
     ids, rec_in, sent_in, tok_in, cot_in, gain_in, down_in, up_in, gd_out, gu_out,
     raw, perm, gn, rec, sent, wd, wu, wdt, wut, xin, xz, uz, xf, fout, bout, red_tx, red_rx,
-    pre, scl, gxz, guz,
+    bred_tx, bred_rx, gt_tx, gt_rx, zed_tx, zed_rx, gt, zed, pre, scl, gxz, guz,
     c_raw, s_tok, s_gn, r_gn, s_tab, r_tab, s_w, r_w, s_x, r_x, s_xr, r_xr,
     s_u, r_u, s_v, r_v, s_vr, r_vr,
-    s_hf, r_hf, s_hb, r_hb, s_red, r_red, s_g, r_g,
+    s_hf, r_hf, s_hb, r_hb, s_red, r_red, s_br, r_br, s_one, r_one, s_g, r_g,
 ):
     s = lax.axis_index("section")
     e = lax.axis_index("dp")
@@ -357,9 +357,6 @@
     table_start(0, 1)
     table_start(1, 1)
     u_forward(2)
-    for k in range(2, 4):
-        table_start(0, k)
-        table_start(1, k)
     for part in range(2):
         pltpu.make_async_copy(gn.at[part], gn.at[part], r_gn.at[part]).wait()
 
@@ -367,6 +364,18 @@
         return pltpu.make_async_remote_copy(
             src_ref=red_tx.at[n], dst_ref=red_rx.at[n], send_sem=s_red.at[n], recv_sem=r_red.at[n],
             device_id=other, device_id_type=MESH,
+        )
+
+    def bred_copy(i):
+        return pltpu.make_async_remote_copy(
+            src_ref=bred_tx.at[i], dst_ref=bred_rx.at[i], send_sem=s_br.at[i], recv_sem=r_br.at[i],
+            device_id=other, device_id_type=MESH,
+        )
+
+    def one_copy(n):
+        src, dst = ((gt_tx, gt_rx), (zed_tx, zed_rx))[n]
+        return pltpu.make_async_remote_copy(
+            src_ref=src, dst_ref=dst, send_sem=s_one.at[n], recv_sem=r_one.at[n], device_id=other, device_id_type=MESH
         )
 
     def col(n):
@@ -439,6 +448,18 @@
 
             lax.fori_loop(0, HALF // CH, one, 0)
 
+        gt_tx[...] = jnp.zeros_like(gt_tx)
+
+        def product(j, carry):
+            at = pl.ds(pl.multiple_of(j * CH, CH), CH)
+            gt_tx[...] += nn((wdt[1, :, at].astype(F32) * gn[1, :, at]).astype(BF16), wut[0, at, :])
+            return carry
+
+        lax.fori_loop(0, HALF // CH, product, 0)
+        one_copy(0).start()
+        one_copy(0).wait_recv()
+        gt[...] = (gt_tx[...] + gt_rx[...]).astype(BF16)
+
     late = z >= STAGES // 2
 
     @pl.when(late)
@@ -452,6 +473,17 @@
         rows = pl.ds(pl.multiple_of(i * TOK, TOK), TOK)
         fresh = jnp.logical_and(i == 0, jnp.logical_not(late))
         table_wait(0, 0, i)
+
+        @pl.when(i == 0)
+        def _():
+            table_start(0, 2)
+            table_start(1, 2)
+
+        @pl.when(i == 2)
+        def _():
+            table_start(0, 3)
+            table_start(1, 3)
+
 
         @pl.when(fresh)
         def _():
@@ -536,6 +568,13 @@
     def _():
         turn()
 
+    zed_tx[...] = jnp.zeros_like(zed_tx)
+    for n in range(NCOL):
+        zed_tx[...] += nn(xz[1, n, :, 0:CH], wut[0, col(n), :])
+    one_copy(1).start()
+    one_copy(1).wait_recv()
+    zed[...] = zed_tx[...] + zed_rx[...]
+
     def early():
         def one(b, carry):
             rows_start(0, b)
@@ -549,7 +588,16 @@
 
     def backward(i, carry):
         rows = pl.ds(pl.multiple_of(i * TOK, TOK), TOK)
-        acc = jnp.zeros((TOK, RANK), F32)
+
+        def slope(part):
+            v = pre[part, rows, :]
+            gate = jax.nn.sigmoid(v)
+            return v, gate * (1.0 + v * (1.0 - gate)), scl[part, rows, 0:1]
+
+        v1, slope1, scale1 = slope(1)
+        v0, slope0, scale0 = slope(0)
+        acc1 = jnp.zeros((TOK, RANK), F32)
+        acc0 = jnp.zeros((TOK, RANK), F32)
         for n in range(NCOL):
             if n % 2 == 0:
                 @pl.when(z < STAGES - 1)
@@ -560,45 +608,37 @@
             def _():
                 uz[1, n, rows, 0:CH] = sent[1, rows, col(n)]
 
-            acc = acc + nn(uz[1, n, rows, 0:CH], wut[1, col(n), :])
-
-        def finish(part, acc):
-            n = 2 * MB + 2 * i + part
-            red_tx[n, :, 0:RANK] = acc
-            red_tx[n, :, RANK:] = jnp.zeros((TOK, 128), F32)
-            red_copy(n).start()
-            red_copy(n).wait_recv()
-            total = acc + red_rx[n, :, 0:RANK]
-            v = pre[part, rows, :]
-            gate = jax.nn.sigmoid(v)
-            d_pre = total * gate * (1.0 + v * (1.0 - gate))
-            scale = scl[part, rows, 0:1]
+            u = uz[1, n, rows, 0:CH]
+            acc1 = acc1 + nn(u, wut[1, col(n), :])
+            acc0 = acc0 + nn(u, wut[0, col(n), :])
+        bred_tx[i, :, 0:RANK] = acc1
+        bred_tx[i, :, RANK:] = acc0
+        bred_copy(i).start()
+        bred_copy(i).wait_recv()
+
+        def finish(d_pre, v, scale):
             mean = jnp.sum(d_pre * v, axis=1, keepdims=True) * (1.0 / D)
-            back = (d_pre * scale).astype(BF16)
-            for j in range(8):
-                uz[part, j, rows, CH:] = back
-            return back, mean * scale * scale
-
-        back, shrink = finish(1, acc)
-        acc = jnp.zeros((TOK, RANK), F32)
+            return (d_pre * scale).astype(BF16), mean * scale * scale
+
+        back1, shrink1 = finish((acc1 + bred_rx[i, :, 0:RANK]) * slope1, v1, scale1)
+        d_act = acc0 + bred_rx[i, :, RANK:] + nn(back1, gt[...]) - shrink1 * zed[rows, :]
+        back0, shrink0 = finish(d_act * slope0, v0, scale0)
         for n in range(NCOL):
             u = (
-                uz[1, n, rows, 0:CH].astype(F32) + nn(back, wdt[1, :, col(n)]) * gn[1, :, col(n)]
-                - shrink * xz[1, n, rows, 0:CH].astype(F32)
+                uz[1, n, rows, 0:CH].astype(F32) + nn(back1, wdt[1, :, col(n)]) * gn[1, :, col(n)]
+                - shrink1 * xz[1, n, rows, 0:CH].astype(F32)
             ).astype(BF16)
             uz[0, n, rows, 0:CH] = u
-            acc = acc + nn(u, wut[0, col(n), :])
-        back, shrink = finish(0, acc)
-
-        @pl.when(z > 0)
-        def _():
-            for n in range(NCOL):
-                u = (
-                    uz[0, n, rows, 0:CH].astype(F32) + nn(back, wdt[0, :, col(n)]) * gn[0, :, col(n)]
-                    - shrink * xz[0, n, rows, 0:CH].astype(F32)
-                )
-                bout[n, rows, :] = u.astype(BF16)
-                if n % 2 == 1:
+            uz[1, n, rows, CH:] = back1
+            uz[0, n, rows, CH:] = back0
+            u = (
+                u.astype(F32) + nn(back0, wdt[0, :, col(n)]) * gn[0, :, col(n)]
+                - shrink0 * xz[0, n, rows, 0:CH].astype(F32)
+            )
+            bout[n, rows, :] = u.astype(BF16)
+            if n % 2 == 1:
+                @pl.when(z > 0)
+                def _():
                     hop(n // 2, i, False).start()
 
         return carry
@@ -658,11 +698,14 @@
             def _():
                 hop(n, i, False).wait_send()
 
-        for k in range(4):
-            red_copy(4 * i + k).wait_send()
+        for k in range(2):
+            red_copy(2 * i + k).wait_send()
+        bred_copy(i).wait_send()
         return carry
 
     lax.fori_loop(0, MB, rest, 0)
+    one_copy(0).wait_send()
+    one_copy(1).wait_send()
 
 
 def shards(tokens, cotangent, sample_ids, sent_before, received_before, norm_gain, down_proj, up_proj):
@@ -693,8 +736,16 @@
             pltpu.VMEM((TOK, HALF), F32),
             pltpu.VMEM((rows, HALF), BF16),
             pltpu.VMEM((8, rows, CH), BF16),
-            pltpu.VMEM((4 * MB, TOK, RANK + 128), F32),
-            pltpu.VMEM((4 * MB, TOK, RANK + 128), F32),
+            pltpu.VMEM((2 * MB, TOK, RANK + 128), F32),
+            pltpu.VMEM((2 * MB, TOK, RANK + 128), F32),
+            pltpu.VMEM((MB, TOK, 2 * RANK), F32),
+            pltpu.VMEM((MB, TOK, 2 * RANK), F32),
+            pltpu.VMEM((RANK, RANK), F32),
+            pltpu.VMEM((RANK, RANK), F32),
+            pltpu.VMEM((rows, RANK), F32),
+            pltpu.VMEM((rows, RANK), F32),
+            pltpu.VMEM((RANK, RANK), BF16),
+            pltpu.VMEM((rows, RANK), F32),
             pltpu.VMEM((2, rows, RANK), F32),
             pltpu.VMEM((2, rows, 128), F32),
             pltpu.VMEM((16 * rows, PACK), BF16),
@@ -706,7 +757,7 @@
             dma((4,)), dma((8,)), dma((4, 4)), dma((2, 4)), dma((2, 4)), dma((4, 2)),
             dma((MB, NCOL // 2)), dma((MB, NCOL // 2)),
             dma((MB, NCOL // 2)), dma((MB, NCOL // 2)),
-            dma((4 * MB,)), dma((4 * MB,)),
+            dma((2 * MB,)), dma((2 * MB,)), dma((MB,)), dma((MB,)), dma((2,)), dma((2,)),
             dma((2, NBATCH, 2, 8)), dma((2, NBATCH, 16)),
         ],
         compiler_params=pltpu.CompilerParams(

time: 302 us -> 277 us (0.917)
  Pallas kernels: 294 us -> 271 us
    pallas_call x1, Pallas kernels: 294 us -> 271 us  [shards(): pl.pallas_call(kernel, out_shape=(jax.ShapeDtypeStruct((CH, RANK), F32),...]
where the time goes in v4:
time: 277 us; the launch traced here: 276 us
  Pallas kernels  271 us (98%)
    pallas_call x1, Pallas kernels, shards(): pl.pallas_call(kernel, out_shape=(jax.ShapeDtypeStruct((CH, RANK), F32),...  271 us

profile of v4, /device:TPU:1, one launch (start us, length us, event | category | flops | bytes accessed | tf_op | source)
XLA Modules:
  0.0 276.4 jit_solution(11134982824725484251)
XLA Ops:
  0.6 0.7 constant_dynamic-slice_fusion
  1.3 271.2 %shard_map.95 = (f32[512,256]{1,0:T(8,128)}, f32[256,512]{1,0:T(8,128)}) custom-call(s32[1,8]{1,0:T(1,128)} %ids.1, bf16[8,16,8192]{2,1,0:T(8,128)(2,1)} %bitcast.8, bf16[8,16,8192]{2,1,0:T(8,128)(2,1)} %bitcast.9, bf16[8,16,8192]{2,1,0:T(8,128)(2,1)} %tok_in.1, bf16[8,16,8192]{2,1,0:T(8,128)(2,1)} %cot_in.1, f32[1,8192]{1,0:T(1,128)} %gain_in.1, ...), custom_call_target="tpu_custom_call" | custom-call | tf_op jit(solution)/shard_map/pallas_call | solution.py:718
  272.5 2.0 multiply_bitcast_fusion
  274.5 1.9 copy.11

commit v5 on v4

--- a/solution.py
+++ b/solution.py
@@ -22,6 +22,7 @@
 BATCH = 2 * TOK
 NBATCH = MB * TOK // BATCH
 PACK = CH + RANK
+LOW = 128
 
 
 def tn(a, b):
@@ -176,33 +177,43 @@
     def away(t):
         return lax.rem(col_x + t, 4)
 
-    def w_remote(t):
-        return pltpu.make_async_remote_copy(
-            src_ref=down_in, dst_ref=wd.at[h, spot, :], send_sem=s_w.at[t], recv_sem=r_w.at[h, c],
+    def shard(kind, part, j):
+        at = pl.ds(pl.multiple_of(j * CH, CH), CH)
+        return wd.at[part, at, :] if kind == 0 else wu.at[part, pl.ds(LOW, RANK - LOW), at]
+
+    def w_remote(kind, t):
+        return pltpu.make_async_remote_copy(
+            src_ref=(down_in, up_in.at[pl.ds(LOW, RANK - LOW), :])[kind], dst_ref=shard(kind, h, slot),
+            send_sem=s_w.at[kind, t], recv_sem=r_w.at[kind, h, c],
             device_id=device(col_x, lax.rem(row_y + t, 4), owner_core), device_id_type=MESH,
         )
 
+    def w_first(kind):
+        @pl.when(local)
+        def _():
+            src = (down_in, up_in.at[pl.ds(LOW, RANK - LOW), :])[kind]
+            pltpu.make_async_copy(src, shard(kind, h, slot), r_w.at[kind, h, c]).start()
+
+        @pl.when(jnp.logical_not(local))
+        def _():
+            w_remote(kind, 0).start()
+
+        for t in (1, 3, 2):
+            w_remote(kind, t).start()
+
     def u_remote(t):
         return pltpu.make_async_remote_copy(
-            src_ref=up_in, dst_ref=wu.at[h, :, spot], send_sem=s_u.at[t], recv_sem=r_u.at[slot],
+            src_ref=up_in.at[pl.ds(0, LOW), :], dst_ref=wu.at[h, pl.ds(0, LOW), spot],
+            send_sem=s_u.at[t], recv_sem=r_u.at[slot],
             device_id=device(away(t), row_y, owner_core), device_id_type=MESH,
         )
 
-    def first_start():
+    def u_first():
         @pl.when(local)
         def _():
-            pltpu.make_async_copy(down_in, wd.at[h, spot, :], r_w.at[h, c]).start()
-
-        @pl.when(jnp.logical_not(local))
-        def _():
-            w_remote(0).start()
-
-        for t in (1, 3, 2):
-            w_remote(t).start()
-
-        @pl.when(local)
-        def _():
-            pltpu.make_async_copy(up_in, wu.at[h, :, spot], r_u.at[slot]).start()
+            pltpu.make_async_copy(
+                up_in.at[pl.ds(0, LOW), :], wu.at[h, pl.ds(0, LOW), spot], r_u.at[slot]
+            ).start()
 
         @pl.when(jnp.logical_not(local))
         def _():
@@ -211,49 +222,61 @@
         for t in (1, 3, 2):
             u_remote(t).start()
 
+    def first_start():
+        w_first(0)
+        u_first()
+        w_first(1)
+
     def first_sent():
         @pl.when(jnp.logical_not(local))
         def _():
-            w_remote(0).wait_send()
+            w_remote(0, 0).wait_send()
+            w_remote(1, 0).wait_send()
             u_remote(0).wait_send()
 
         for t in range(1, 4):
-            w_remote(t).wait_send()
+            w_remote(0, t).wait_send()
+            w_remote(1, t).wait_send()
             u_remote(t).wait_send()
 
-    def w_block(part, t):
-        place = wd.at[part, wide(col_x), :]
-        return pltpu.make_async_remote_copy(
-            src_ref=place, dst_ref=place, send_sem=s_x.at[part, t], recv_sem=r_x.at[part, col_x],
+    def w_place(kind, part, x):
+        return wd.at[part, wide(x), :] if kind == 0 else wu.at[part, pl.ds(LOW, RANK - LOW), wide(x)]
+
+    def w_block(kind, part, t):
+        place = w_place(kind, part, col_x)
+        return pltpu.make_async_remote_copy(
+            src_ref=place, dst_ref=place, send_sem=s_x.at[kind, part, t], recv_sem=r_x.at[kind, part, col_x],
             device_id=(s, e - 2 * col_x + 2 * away(t)), device_id_type=MESH,
         )
 
-    def w_start(part):
+    def w_start(kind, part):
         for j in range(2):
-            place = wd.at[part, pl.ds(pl.multiple_of((2 * col_x + j) * CH, CH), CH), :]
-            pltpu.make_async_copy(place, place, r_w.at[part, j]).wait()
+            place = shard(kind, part, 2 * col_x + j)
+            pltpu.make_async_copy(place, place, r_w.at[kind, part, j]).wait()
         for t in (1, 3):
-            w_block(part, t).start()
-
-    def w_half(part, x, half):
-        return wd.at[part, pl.ds(pl.multiple_of((2 * x + half) * CH, CH), CH), :]
-
-    def w_relay(part, half):
-        place = w_half(part, away((3, 1)[half]), half)
-        return pltpu.make_async_remote_copy(
-            src_ref=place, dst_ref=place, send_sem=s_xr.at[part, half], recv_sem=r_xr.at[part, half],
+            w_block(kind, part, t).start()
+
+    def w_half(kind, part, x, half):
+        if kind == 0:
+            return wd.at[part, pl.ds(pl.multiple_of((2 * x + half) * CH, CH), CH), :]
+        return wu.at[part, pl.ds(LOW + half * ((RANK - LOW) // 2), (RANK - LOW) // 2), wide(x)]
+
+    def w_relay(kind, part, half):
+        place = w_half(kind, part, away((3, 1)[half]), half)
+        return pltpu.make_async_remote_copy(
+            src_ref=place, dst_ref=place, send_sem=s_xr.at[kind, part, half], recv_sem=r_xr.at[kind, part, half],
             device_id=(s, e - 2 * col_x + 2 * away((1, 3)[half])), device_id_type=MESH,
         )
 
-    def w_forward(part):
+    def w_forward(kind, part):
         for half in range(2):
             x = away((3, 1)[half])
-            place = wd.at[part, wide(x), :]
-            pltpu.make_async_copy(place, place, r_x.at[part, x]).wait()
-            w_relay(part, half).start()
+            place = w_place(kind, part, x)
+            pltpu.make_async_copy(place, place, r_x.at[kind, part, x]).wait()
+            w_relay(kind, part, half).start()
 
     def u_block(n, t):
-        place = wu.at[h, :, wide(away(n))]
+        place = wu.at[h, pl.ds(0, LOW), wide(away(n))]
         return pltpu.make_async_remote_copy(
             src_ref=place, dst_ref=place, send_sem=s_v.at[n, t], recv_sem=r_v.at[h, away(n)],
             device_id=device(col_x, lax.rem(row_y + t, 4), c), device_id_type=MESH,
@@ -264,7 +287,7 @@
         def _():
             for j in range(2):
                 at = 2 * away(n) + j
-                place = wu.at[h, :, pl.ds(pl.multiple_of(at * CH, CH), CH)]
+                place = wu.at[h, pl.ds(0, LOW), pl.ds(pl.multiple_of(at * CH, CH), CH)]
                 pltpu.make_async_copy(place, place, r_u.at[at]).wait()
             for t in (1, 3):
                 u_block(n, t).start()
@@ -272,7 +295,7 @@
     y_me = 2 * h + lax.div(e, 8)
 
     def u_half(part, n, half):
-        return wu.at[part, pl.ds(pl.multiple_of(half * (RANK // 2), RANK // 2), RANK // 2), wide(away(n))]
+        return wu.at[part, pl.ds(pl.multiple_of(half * (LOW // 2), LOW // 2), LOW // 2), wide(away(n))]
 
     def u_relay(part, n):
         half = jnp.where(lax.rem(y_me - 2 * part - c + 4, 4) == 1, 0, 1)
@@ -286,16 +309,15 @@
         @pl.when(jnp.logical_not(local))
         def _():
             for part in range(2):
-                place = wu.at[part, :, wide(away(n))]
+                place = wu.at[part, pl.ds(0, LOW), wide(away(n))]
                 pltpu.make_async_copy(place, place, r_v.at[part, away(n)]).wait()
                 u_relay(part, n).start()
 
     def weight_wait(kind, part):
-        if kind == 0:
-            for half in range(2):
-                place = w_half(part, away(2), half)
-                pltpu.make_async_copy(place, place, r_xr.at[part, half]).wait()
-        else:
+        for half in range(2):
+            place = w_half(kind, part, away(2), half)
+            pltpu.make_async_copy(place, place, r_xr.at[kind, part, half]).wait()
+        if kind == 1:
             @pl.when(jnp.logical_and(local, h != part))
             def _():
                 for n in range(4):
@@ -305,11 +327,12 @@
 
     def weight_sent():
         first_sent()
-        for part in range(2):
-            for t in (1, 3):
-                w_block(part, t).wait_send()
-            for half in range(2):
-                w_relay(part, half).wait_send()
+        for kind in range(2):
+            for part in range(2):
+                for t in (1, 3):
+                    w_block(kind, part, t).wait_send()
+                for half in range(2):
+                    w_relay(kind, part, half).wait_send()
 
         @pl.when(local)
         def _():
@@ -344,19 +367,23 @@
     def _():
         end_start(1)
 
-    w_start(0)
+    w_start(0, h)
     u_start(0)
-    w_start(1)
+    w_start(1, h)
+    w_start(0, 1 - h)
+    w_start(1, 1 - h)
     for n in (1, 3, 2):
         u_start(n)
-    w_forward(0)
+    w_forward(0, h)
     u_forward(0)
-    w_forward(1)
+    w_forward(1, h)
     u_forward(1)
-    u_forward(3)
     table_start(0, 1)
     table_start(1, 1)
+    u_forward(3)
+    w_forward(0, 1 - h)
     u_forward(2)
+    w_forward(1, 1 - h)
     for part in range(2):
         pltpu.make_async_copy(gn.at[part], gn.at[part], r_gn.at[part]).wait()
 
@@ -753,7 +780,7 @@
             dma, dma((4,)),
             dma, dma((2,)),
             dma((2, 4, 4)), dma((2, 2, MB)),
-            dma((4,)), dma((2, 2)), dma((2, 4)), dma((2, 4)), dma((2, 2)), dma((2, 2)),
+            dma((2, 4)), dma((2, 2, 2)), dma((2, 2, 4)), dma((2, 2, 4)), dma((2, 2, 2)), dma((2, 2, 2)),
             dma((4,)), dma((8,)), dma((4, 4)), dma((2, 4)), dma((2, 4)), dma((4, 2)),
             dma((MB, NCOL // 2)), dma((MB, NCOL // 2)),
             dma((MB, NCOL // 2)), dma((MB, NCOL // 2)),

time: 277 us -> 266 us (0.960)
  Pallas kernels: 271 us -> 261 us
    pallas_call x1, Pallas kernels: 271 us -> 261 us  [shards(): pl.pallas_call(kernel, out_shape=(jax.ShapeDtypeStruct((CH, RANK), F32),...]
where the time goes in v5:
time: 266 us
  Pallas kernels  261 us (98%)
    pallas_call x1, Pallas kernels, shards(): pl.pallas_call(kernel, out_shape=(jax.ShapeDtypeStruct((CH, RANK), F32),...  261 us

profile of v5, /device:TPU:1, one launch (start us, length us, event | category | flops | bytes accessed | tf_op | source)
XLA Modules:
  0.0 266.1 jit_solution(13640716175117022362)
XLA Ops:
  0.6 0.7 constant_dynamic-slice_fusion
  1.3 260.9 %shard_map.95 = (f32[512,256]{1,0:T(8,128)}, f32[256,512]{1,0:T(8,128)}) custom-call(s32[1,8]{1,0:T(1,128)} %ids.1, bf16[8,16,8192]{2,1,0:T(8,128)(2,1)} %bitcast.8, bf16[8,16,8192]{2,1,0:T(8,128)(2,1)} %bitcast.9, bf16[8,16,8192]{2,1,0:T(8,128)(2,1)} %tok_in.1, bf16[8,16,8192]{2,1,0:T(8,128)(2,1)} %cot_in.1, f32[1,8192]{1,0:T(1,128)} %gain_in.1, ...), custom_call_target="tpu_custom_call" | custom-call | tf_op jit(solution)/shard_map/pallas_call | solution.py:745
  262.3 2.0 multiply_bitcast_fusion
  264.2 1.9 copy.11

commit v6 on v5

--- a/solution.py
+++ b/solution.py
@@ -449,7 +449,7 @@
 
             return carry
 
-        lax.fori_loop(0, 16, one, 0)
+        lax.fori_loop(0, 16, one, 0, unroll=4)
 
     def rows_start(kind, b):
         rows_each(kind, b, True, lambda copy: copy.start())
@@ -599,8 +599,6 @@
     for n in range(NCOL):
         zed_tx[...] += nn(xz[1, n, :, 0:CH], wut[0, col(n), :])
     one_copy(1).start()
-    one_copy(1).wait_recv()
-    zed[...] = zed_tx[...] + zed_rx[...]
 
     def early():
         def one(b, carry):
@@ -641,6 +639,12 @@
         bred_tx[i, :, 0:RANK] = acc1
         bred_tx[i, :, RANK:] = acc0
         bred_copy(i).start()
+
+        @pl.when(i == 0)
+        def _():
+            one_copy(1).wait_recv()
+            zed[...] = zed_tx[...] + zed_rx[...]
+
         bred_copy(i).wait_recv()
 
         def finish(d_pre, v, scale):
@@ -681,6 +685,51 @@
     def _():
         early()
 
+    weight_sent()
+    gain_far.wait_send()
+
+    @pl.when(z == 0)
+    def _():
+        end_sent(0)
+
+    @pl.when(z == STAGES - 1)
+    def _():
+        end_sent(1)
+
+    for k in range(4):
+        table_sent(0, k)
+        table_sent(1, k)
+
+    def rest(i, carry):
+        for n in range(NCOL // 2):
+            @pl.when(z < STAGES - 1)
+            def _():
+                hop(n, i, True).wait_send()
+
+            @pl.when(z > 0)
+            def _():
+                hop(n, i, False).wait_send()
+
+        for k in range(2):
+            red_copy(2 * i + k).wait_send()
+        bred_copy(i).wait_send()
+        return carry
+
+    lax.fori_loop(0, MB, rest, 0)
+    one_copy(0).wait_send()
+    one_copy(1).wait_send()
+
+    def rows_gone(b, carry):
+        rows_sent(0, b)
+
+        @pl.when(b < NBATCH - 1)
+        def _():
+            rows_sent(1, b)
+
+        return carry
+
+    lax.fori_loop(0, NBATCH, rows_gone, 0)
+
     gd_out[...] = jnp.zeros_like(gd_out)
     gu_out[...] = jnp.zeros_like(gu_out)
 
@@ -693,46 +742,7 @@
         return carry
 
     lax.fori_loop(0, NBATCH, total, 0)
-
-    def all_rows_sent(b, carry):
-        rows_sent(0, b)
-        rows_sent(1, b)
-        return carry
-
-    lax.fori_loop(0, NBATCH, all_rows_sent, 0)
-    weight_sent()
-    gain_far.wait_send()
-
-    @pl.when(z == 0)
-    def _():
-        end_sent(0)
-
-    @pl.when(z == STAGES - 1)
-    def _():
-        end_sent(1)
-
-    for k in range(4):
-        table_sent(0, k)
-        table_sent(1, k)
-
-    def rest(i, carry):
-        for n in range(NCOL // 2):
-            @pl.when(z < STAGES - 1)
-            def _():
-                hop(n, i, True).wait_send()
-
-            @pl.when(z > 0)
-            def _():
-                hop(n, i, False).wait_send()
-
-        for k in range(2):
-            red_copy(2 * i + k).wait_send()
-        bred_copy(i).wait_send()
-        return carry
-
-    lax.fori_loop(0, MB, rest, 0)
-    one_copy(0).wait_send()
-    one_copy(1).wait_send()
+    rows_sent(1, NBATCH - 1)
 
 
 def shards(tokens, cotangent, sample_ids, sent_before, received_before, norm_gain, down_proj, up_proj):

time: 266 us -> 263 us (0.989)
  Pallas kernels: 261 us -> 258 us
    pallas_call x1, Pallas kernels: 261 us -> 258 us  [shards(): pl.pallas_call(kernel, out_shape=(jax.ShapeDtypeStruct((CH, RANK), F32),...]
where the time goes in v6:
time: 263 us
  Pallas kernels  258 us (98%)
    pallas_call x1, Pallas kernels, shards(): pl.pallas_call(kernel, out_shape=(jax.ShapeDtypeStruct((CH, RANK), F32),...  258 us

profile of v6, /device:TPU:1, one launch (start us, length us, event | category | flops | bytes accessed | tf_op | source)
XLA Modules:
  0.0 263.2 jit_solution(6239980774067632265)
XLA Ops:
  0.6 0.7 constant_dynamic-slice_fusion
  1.3 258.0 %shard_map.95 = (f32[512,256]{1,0:T(8,128)}, f32[256,512]{1,0:T(8,128)}) custom-call(s32[1,8]{1,0:T(1,128)} %ids.1, bf16[8,16,8192]{2,1,0:T(8,128)(2,1)} %bitcast.8, bf16[8,16,8192]{2,1,0:T(8,128)(2,1)} %bitcast.9, bf16[8,16,8192]{2,1,0:T(8,128)(2,1)} %tok_in.1, bf16[8,16,8192]{2,1,0:T(8,128)(2,1)} %cot_in.1, f32[1,8192]{1,0:T(1,128)} %gain_in.1, ...), custom_call_target="tpu_custom_call" | custom-call | tf_op jit(solution)/shard_map/pallas_call | solution.py:755
  259.3 2.0 multiply_bitcast_fusion
  261.3 1.9 copy.11

commit v7 on v6

--- a/solution.py
+++ b/solution.py
@@ -660,8 +660,6 @@
                 - shrink1 * xz[1, n, rows, 0:CH].astype(F32)
             ).astype(BF16)
             uz[0, n, rows, 0:CH] = u
-            uz[1, n, rows, CH:] = back1
-            uz[0, n, rows, CH:] = back0
             u = (
                 u.astype(F32) + nn(back0, wdt[0, :, col(n)]) * gn[0, :, col(n)]
                 - shrink0 * xz[0, n, rows, 0:CH].astype(F32)
@@ -672,6 +670,9 @@
                 def _():
                     hop(n // 2, i, False).start()
 
+        for n in range(NCOL):
+            uz[1, n, rows, CH:] = back1
+            uz[0, n, rows, CH:] = back0
         return carry
 
     def back_batch(b, carry):

time: 263 us -> 264 us (level)
  no operation moved by 1% of the time
where the time goes in v7:
time: 264 us; the launch traced here: 263 us
  Pallas kernels  258 us (98%)
    pallas_call x1, Pallas kernels, shards(): pl.pallas_call(kernel, out_shape=(jax.ShapeDtypeStruct((CH, RANK), F32),...  258 us

profile of v7, /device:TPU:1, one launch (start us, length us, event | category | flops | bytes accessed | tf_op | source)
XLA Modules:
  0.0 263.3 jit_solution(17450995300120618415)
XLA Ops:
  0.6 0.7 constant_dynamic-slice_fusion
  1.3 258.1 %shard_map.95 = (f32[512,256]{1,0:T(8,128)}, f32[256,512]{1,0:T(8,128)}) custom-call(s32[1,8]{1,0:T(1,128)} %ids.1, bf16[8,16,8192]{2,1,0:T(8,128)(2,1)} %bitcast.8, bf16[8,16,8192]{2,1,0:T(8,128)(2,1)} %bitcast.9, bf16[8,16,8192]{2,1,0:T(8,128)(2,1)} %tok_in.1, bf16[8,16,8192]{2,1,0:T(8,128)(2,1)} %cot_in.1, f32[1,8192]{1,0:T(1,128)} %gain_in.1, ...), custom_call_target="tpu_custom_call" | custom-call | tf_op jit(solution)/shard_map/pallas_call | solution.py:756
  259.5 2.0 multiply_bitcast_fusion
  261.4 1.9 copy.11
